TPU v7x, 32 devices: a whole 2x2x4 slice. The times are simulated.
32 devices in a mesh: node: 4 (over y, core), rows: 8 (over z, x).
Axes of the slice: x: 2, y: 2, z: 4, core: 2. Of those that a mesh axis runs over, the one named last changes fastest.
Arguments:
- columns: bfloat16 [32, 192, 128], P(None, 'rows'), may hold values from -6 to 6
- pencil_e: bfloat16 [192, 5, 128, 128], P('rows'), may hold values from -2 to 3, as said below
- pencil_a: bfloat16 [192, 5, 128, 128], P('rows'), may hold values from -5 to 2, as said below
- precond: bfloat16 [4, 2, 192, 128, 128], P('node', None, 'rows'), may hold values from -30 to 30, as said below
- neighbours: int32 [192, 5], P('rows'), may hold values from 0 to 191, as said below
Outputs:
- projected: float32 [2, 32, 192, 128], P(None, 'node', 'rows')
Inputs may be any that keep to these rules, and one draw needn't show every extreme that they name: neighbours[i, 0] = i. Every entry lies in the block rows of a device whose index along rows is at most 2 away, or exactly half of the 8 devices away, counted around the cycle. For each device and each other device, at most 6 entries of the first one's block rows lie in the second one's block rows; every device has exactly 6 entries in the block rows of the device half the cycle away. `pencil_e`: slot 0 holds the diagonal block. `pencil_a`: slot 0 holds the diagonal block. precond[k, 0, i] + i precond[k, 1, i] is the inverse of z_k E_i - A_i, where E_i and A_i are the float32 diagonal blocks before they were rounded to give pencil_e[i, 0] and pencil_a[i, 0]; the inverse is then rounded to bfloat16.
All inputs are finite; a program needn't handle non-finite values.
Results may differ from a plain program's by a relative error of at most 0.0017.
Values may be sent and summed in bfloat16 or wider, within the bound.
A program may use at most 64 MiB of HBM per device.

v0:
```python
import math

import jax
import jax.numpy as jnp
from jax import lax
from jax.sharding import PartitionSpec as P

SLOTS = 5
HMAX = 6
REACH = 2
SWEEPS = 2


def from_behind(value, axis, by):
    devices = lax.axis_size(axis)
    return lax.ppermute(value, axis, [(i, (i + by) % devices) for i in range(devices)])


def apply_blocks(extended, matrices, slot_index, dev_rows):
    summed = jnp.zeros((extended.shape[0], dev_rows, extended.shape[2]), jnp.float32)
    for slot in range(SLOTS):
        picked = extended[:, slot_index[:, slot], :]
        summed = summed + jnp.einsum(
            "cnb,nbd->cnd", picked, matrices[:, slot], preferred_element_type=jnp.float32
        )
    return summed


def precondition(residual, inverse):
    products = jnp.einsum("pcnb,mnbd->pmcnd", residual, inverse, preferred_element_type=jnp.float32)
    return jnp.stack([products[0, 0] - products[1, 1], products[0, 1] + products[1, 0]])


def per_device(columns, pencil_e, pencil_a, precond, neighbours):
    dev_rows = pencil_e.shape[0]
    block_size = pencil_e.shape[2]
    col_count = columns.shape[0]
    peer_count = lax.axis_size("rows")
    my_index = lax.axis_index("rows")
    owners = neighbours // dev_rows
    local_ids = neighbours - owners * dev_rows
    entries = dev_rows * SLOTS
    flat_owner = owners.reshape(-1)
    flat_local = local_ids.reshape(-1)
    flat_remote = flat_owner != my_index
    position = jnp.arange(entries)
    earlier = (
        (flat_owner[None, :] == flat_owner[:, None])
        & flat_remote[None, :]
        & (position[None, :] < position[:, None])
    )
    slot_rank = jnp.sum(earlier, axis=1)
    rank_range = jnp.arange(HMAX)
    half_cycle = peer_count // 2
    signed_off = (flat_owner - my_index + peer_count) % peer_count
    far_link = signed_off == half_cycle
    signed_off = jnp.where(signed_off > half_cycle, signed_off - peer_count, signed_off)
    lane = jnp.where(signed_off < 0, signed_off + REACH, signed_off + REACH - 1)
    lane = jnp.where(far_link, 2 * REACH, lane)
    slot_flat = jnp.where(flat_remote, dev_rows + lane * HMAX + slot_rank, flat_local)
    offsets = list(range(-REACH, 0)) + list(range(1, REACH + 1)) + [half_cycle]
    asked_lists = []
    for offset in offsets:
        matched = (
            flat_remote[None, :]
            & (signed_off[None, :] == offset)
            & (slot_rank[None, :] == rank_range[:, None])
        )
        wanted = jnp.sum(jnp.where(matched, flat_local[None, :], 0), axis=1)
        asked_lists.append(from_behind(wanted, "rows", offset))

    def fetch_halo(vector):
        pieces = [vector]
        for offset, asked_for in zip(offsets, asked_lists):
            outgoing = vector[:, asked_for, :]
            pieces.append(from_behind(outgoing, "rows", -offset))
        return jnp.concatenate(pieces, axis=1)

    slot_index = slot_flat.reshape(dev_rows, SLOTS)
    rhs_full = apply_blocks(fetch_halo(columns), pencil_e, slot_index, dev_rows)
    node_count = lax.axis_size("node")
    angle_node = 2.0 * math.pi * (lax.axis_index("node").astype(jnp.float32) + 0.5) / node_count
    node_real = jnp.cos(angle_node)
    node_imag = jnp.sin(angle_node)
    inverse = precond[0]
    rhs_round = rhs_full.astype(jnp.bfloat16)
    iterate = jnp.einsum("cnb,mnbd->mcnd", rhs_round, inverse, preferred_element_type=jnp.float32)
    for sweep_step in range(SWEEPS):
        rounded = iterate.astype(jnp.bfloat16).reshape(2 * col_count, dev_rows, block_size)
        extended = fetch_halo(rounded)
        with_e = apply_blocks(extended, pencil_e, slot_index, dev_rows).reshape(
            2, col_count, dev_rows, block_size
        )
        with_a = apply_blocks(extended, pencil_a, slot_index, dev_rows).reshape(
            2, col_count, dev_rows, block_size
        )
        applied_real = node_real * with_e[0] - node_imag * with_e[1] - with_a[0]
        applied_imag = node_real * with_e[1] + node_imag * with_e[0] - with_a[1]
        residual = jnp.stack([rhs_full - applied_real, -applied_imag]).astype(jnp.bfloat16)
        iterate = iterate + precondition(residual, inverse)
    weighted = jnp.stack(
        [
            node_real * iterate[0] - node_imag * iterate[1],
            node_real * iterate[1] + node_imag * iterate[0],
        ]
    )
    weighted = weighted / node_count
    return lax.psum_scatter(weighted, "node", scatter_dimension=1, tiled=True)


def solution(mesh):
    placed = (
        P(None, "rows", None),
        P("rows", None, None, None),
        P("rows", None, None, None),
        P("node", None, "rows", None, None),
        P("rows", None),
    )
    return jax.shard_map(
        per_device,
        mesh=mesh,
        in_specs=placed,
        out_specs=P(None, "node", "rows", None),
        check_vma=False,
    )
```

profile of v0, /device:TPU:0, one launch (start us, length us, event | category | flops | bytes accessed | tf_op | source)
XLA Modules:
  0.0 154.3 jit_solution(6342783287435628943)
XLA Ops:
  8.2 3.0 %collective-permute-start.4 = (s32[6]{0:T(128)S(1)}, s32[6]{0:T(128)S(1)}, u32[]{:S(2)}, u32[]{:S(2)}) collective-permute-start(s32[6]{0:T(128)S(1)} %get-tuple-element.12), channel_id=1, source_target_pairs={{0,1},{1,2},{2,3},{3,4},{4,5},{5,6},{6,7},{7,0},{8,9},{9,10},{10,1... | collective-permute-start | bytes 80 | tf_op jit(solution)/shard_map/ppermute | solution.py:16
  11.2 3.1 %collective-permute-start.2 = (s32[6]{0:T(128)S(1)}, s32[6]{0:T(128)S(1)}, u32[]{:S(2)}, u32[]{:S(2)}) collective-permute-start(s32[6]{0:T(128)S(1)} %get-tuple-element.11), channel_id=1, source_target_pairs={{0,7},{1,0},{2,1},{3,2},{4,3},{5,4},{6,5},{7,6},{8,15},{9,8},{10,9... | collective-permute-start | bytes 80 | tf_op jit(solution)/shard_map/ppermute | solution.py:16
  14.3 1.9 %collective-permute-start = (s32[6]{0:T(128)S(1)}, s32[6]{0:T(128)S(1)}, u32[]{:S(2)}, u32[]{:S(2)}) collective-permute-start(s32[6]{0:T(128)S(1)} %get-tuple-element.14), channel_id=1, source_target_pairs={{0,6},{1,7},{2,0},{3,1},{4,2},{5,3},{6,4},{7,5},{8,14},{9,15},{10,... | collective-permute-start | bytes 80 | tf_op jit(solution)/shard_map/ppermute | solution.py:16
  18.7 1.7 %gather_fusion.1 = bf16[6,32,128]{2,0,1:T(8,128)(2,1)S(1)} fusion(bf16[32,24,128]{2,1,0:T(8,128)(2,1)} %param.5, s32[1024]{0:T(1024)S(1)} %get-tuple-element.43), kind=kCustom, calls=%fused_computation.1 | custom fusion | bytes 98328 | tf_op jit(solution)/shard_map/gather | solution.py:75
  21.1 1.7 %gather_fusion = bf16[6,32,128]{2,0,1:T(8,128)(2,1)S(1)} fusion(bf16[32,24,128]{2,1,0:T(8,128)(2,1)} %param.5, s32[1024]{0:T(1024)S(1)} %pad_clamp_fusion.9), kind=kCustom, calls=%fused_computation | custom fusion | bytes 98328 | tf_op jit(solution)/shard_map/gather | solution.py:75
  22.8 2.5 %collective-permute-start.1 = (bf16[32,6,128]{2,1,0:T(8,128)(2,1)S(1)}, bf16[32,6,128]{2,1,0:T(8,128)(2,1)S(1)}, u32[]{:S(2)}, u32[]{:S(2)}) collective-permute-start(bf16[32,6,128]{2,1,0:T(8,128)(2,1)S(1)} %bitcast.250), channel_id=1, source_target_pairs={{0,2},{1,3},{2,4},{3,5},{4,6},{5,7},{6,0},{7,1},{8,10},{9,11},{10,... | collective-permute-start | bytes 147464 | tf_op jit(solution)/shard_map/ppermute | solution.py:16
  25.3 1.7 %gather_fusion.2 = bf16[6,32,128]{2,0,1:T(8,128)(2,1)S(1)} fusion(bf16[32,24,128]{2,1,0:T(8,128)(2,1)} %param.5, s32[1024]{0:T(1024)S(1)} %get-tuple-element.42), kind=kCustom, calls=%fused_computation.2 | custom fusion | bytes 98328 | tf_op jit(solution)/shard_map/gather | solution.py:75
  27.0 4.2 %collective-permute-start.5 = (bf16[32,6,128]{2,1,0:T(8,128)(2,1)S(1)}, bf16[32,6,128]{2,1,0:T(8,128)(2,1)S(1)}, u32[]{:S(2)}, u32[]{:S(2)}) collective-permute-start(bf16[32,6,128]{2,1,0:T(8,128)(2,1)S(1)} %bitcast.249), channel_id=1, source_target_pairs={{0,7},{1,0},{2,1},{3,2},{4,3},{5,4},{6,5},{7,6},{8,15},{9,8},{10,9... | collective-permute-start | bytes 147464 | tf_op jit(solution)/shard_map/ppermute | solution.py:16
  31.2 1.7 %gather_fusion.3 = bf16[6,32,128]{2,0,1:T(8,128)(2,1)S(1)} fusion(bf16[32,24,128]{2,1,0:T(8,128)(2,1)} %param.5, s32[1024]{0:T(1024)S(1)} %get-tuple-element.41), kind=kCustom, calls=%fused_computation.3 | custom fusion | bytes 98328 | tf_op jit(solution)/shard_map/gather | solution.py:75
  33.0 1.7 %gather_fusion.4 = bf16[6,32,128]{2,0,1:T(8,128)(2,1)S(1)} fusion(bf16[32,24,128]{2,1,0:T(8,128)(2,1)} %param.5, s32[1024]{0:T(1024)S(1)} %get-tuple-element.40), kind=kCustom, calls=%fused_computation.4 | custom fusion | bytes 98328 | tf_op jit(solution)/shard_map/gather | solution.py:75
  34.8 2.4 %collective-permute-done.7 = bf16[32,6,128]{2,1,0:T(8,128)(2,1)S(1)} collective-permute-done((bf16[32,6,128]{2,1,0:T(8,128)(2,1)S(1)}, bf16[32,6,128]{2,1,0:T(8,128)(2,1)S(1)}, u32[]{:S(2)}, u32[]{:S(2)}) %collective-permute-start.7) | collective-permute-done | bytes 49184 | tf_op jit(solution)/shard_map/ppermute | solution.py:16
  37.2 2.6 %collective-permute-done.9 = bf16[32,6,128]{2,1,0:T(8,128)(2,1)S(1)} collective-permute-done((bf16[32,6,128]{2,1,0:T(8,128)(2,1)S(1)}, bf16[32,6,128]{2,1,0:T(8,128)(2,1)S(1)}, u32[]{:S(2)}, u32[]{:S(2)}) %collective-permute-start.9) | collective-permute-done | bytes 49184 | tf_op jit(solution)/shard_map/ppermute | solution.py:16
  55.5 2.1 %collective-permute-start.10 = (bf16[64,6,128]{2,0,1:T(8,128)(2,1)}, bf16[64,6,128]{2,0,1:T(8,128)(2,1)S(1)}, u32[]{:S(2)}, u32[]{:S(2)}) collective-permute-start(bf16[64,6,128]{2,0,1:T(8,128)(2,1)} %bitcast.21), channel_id=1, source_target_pairs={{0,2},{1,3},{2,4},{3,5},{4,6},{5,7},{6,0},{7,1},{8,10},{9,11},{10,... | collective-permute-start | bytes 294920 | tf_op jit(solution)/shard_map/ppermute | solution.py:16
  57.6 4.7 %collective-permute-start.12 = (bf16[64,6,128]{2,0,1:T(8,128)(2,1)S(1)}, bf16[64,6,128]{2,0,1:T(8,128)(2,1)S(1)}, u32[]{:S(2)}, u32[]{:S(2)}) collective-permute-start(bf16[64,6,128]{2,0,1:T(8,128)(2,1)S(1)} %bitcast.247), channel_id=1, source_target_pairs={{0,7},{1,0},{2,1},{3,2},{4,3},{5,4},{6,5},{7,6},{8,15},{9,8},{10,9... | collective-permute-start | bytes 294920 | tf_op jit(solution)/shard_map/ppermute | solution.py:16
  63.4 1.9 %collective-permute-done.11 = bf16[64,6,128]{2,0,1:T(8,128)(2,1)S(1)} collective-permute-done((bf16[64,6,128]{2,0,1:T(8,128)(2,1)}, bf16[64,6,128]{2,0,1:T(8,128)(2,1)S(1)}, u32[]{:S(2)}, u32[]{:S(2)}) %collective-permute-start.11) | collective-permute-done | bytes 98336 | tf_op jit(solution)/shard_map/ppermute | solution.py:16
  65.3 2.7 %collective-permute-done.13 = bf16[64,6,128]{2,0,1:T(8,128)(2,1)S(1)} collective-permute-done((bf16[64,6,128]{2,0,1:T(8,128)(2,1)S(1)}, bf16[64,6,128]{2,0,1:T(8,128)(2,1)S(1)}, u32[]{:S(2)}, u32[]{:S(2)}) %collective-permute-start.13) | collective-permute-done | bytes 98336 | tf_op jit(solution)/shard_map/ppermute | solution.py:16
  69.5 1.5 gather_fusion.17
  71.0 1.5 gather_fusion.16
  75.5 1.7 %fusion.57 = f32[24,64,128]{2,1,0:T(8,128)S(1)} fusion(bf16[24,5,128,128]{3,2,1,0:T(8,128)(2,1)} %param.6, bf16[24,64,128]{2,1,0:T(8,128)(2,1)} %gather_fusion.18), kind=kOutput, calls=%fused_computation.92 | convolution fusion | flops 50331648 | bytes 1966080 | tf_op jit(solution)/shard_map/cnb,nbd->cnd/dot_general | solution.py:23
  77.2 1.7 %fusion.62 = f32[24,64,128]{2,1,0:T(8,128)S(1)} fusion(bf16[24,5,128,128]{3,2,1,0:T(8,128)(2,1)} %param.6, bf16[24,64,128]{2,1,0:T(8,128)(2,1)} %gather_fusion.17), kind=kOutput, calls=%fused_computation.97 | convolution fusion | flops 50331648 | bytes 1966080 | tf_op jit(solution)/shard_map/cnb,nbd->cnd/dot_general | solution.py:23
  79.0 1.6 %fusion.38 = f32[24,64,128]{2,1,0:T(8,128)S(1)} fusion(bf16[24,5,128,128]{3,2,1,0:T(8,128)(2,1)} %param.7, bf16[24,64,128]{2,1,0:T(8,128)(2,1)} %gather_fusion.18), kind=kOutput, calls=%fused_computation.73 | convolution fusion | flops 50331648 | bytes 1966080 | tf_op jit(solution)/shard_map/cnb,nbd->cnd/dot_general | solution.py:23
  90.5 1.9 %collective-permute-start.15 = (bf16[64,6,128]{2,0,1:T(8,128)(2,1)}, bf16[64,6,128]{2,0,1:T(8,128)(2,1)S(1)}, u32[]{:S(2)}, u32[]{:S(2)}) collective-permute-start(bf16[64,6,128]{2,0,1:T(8,128)(2,1)} %bitcast.47), channel_id=1, source_target_pairs={{0,2},{1,3},{2,4},{3,5},{4,6},{5,7},{6,0},{7,1},{8,10},{9,11},{10,... | collective-permute-start | bytes 294920 | tf_op jit(solution)/shard_map/ppermute | solution.py:16
  92.4 4.7 %collective-permute-start.17 = (bf16[64,6,128]{2,0,1:T(8,128)(2,1)S(1)}, bf16[64,6,128]{2,0,1:T(8,128)(2,1)S(1)}, u32[]{:S(2)}, u32[]{:S(2)}) collective-permute-start(bf16[64,6,128]{2,0,1:T(8,128)(2,1)S(1)} %bitcast.246), channel_id=1, source_target_pairs={{0,7},{1,0},{2,1},{3,2},{4,3},{5,4},{6,5},{7,6},{8,15},{9,8},{10,9... | collective-permute-start | bytes 294920 | tf_op jit(solution)/shard_map/ppermute | solution.py:16
  100.1 1.7 %collective-permute-done.18 = bf16[64,6,128]{2,0,1:T(8,128)(2,1)S(1)} collective-permute-done((bf16[64,6,128]{2,0,1:T(8,128)(2,1)S(1)}, bf16[64,6,128]{2,0,1:T(8,128)(2,1)S(1)}, u32[]{:S(2)}, u32[]{:S(2)}) %collective-permute-start.18) | collective-permute-done | bytes 98336 | tf_op jit(solution)/shard_map/ppermute | solution.py:16
  102.9 1.5 gather_fusion.28
  104.4 1.5 gather_fusion.27
  107.4 1.5 gather_fusion.29
  110.4 1.7 %fusion.55 = f32[24,64,128]{2,1,0:T(8,128)S(1)} fusion(bf16[24,5,128,128]{3,2,1,0:T(8,128)(2,1)} %param.6, bf16[24,64,128]{2,1,0:T(8,128)(2,1)} %gather_fusion.28), kind=kOutput, calls=%fused_computation.90 | convolution fusion | flops 50331648 | bytes 1966080 | tf_op jit(solution)/shard_map/cnb,nbd->cnd/dot_general | solution.py:23
  112.1 1.7 %fusion.36 = f32[24,64,128]{2,1,0:T(8,128)S(1)} fusion(bf16[24,5,128,128]{3,2,1,0:T(8,128)(2,1)} %param.7, bf16[24,64,128]{2,1,0:T(8,128)(2,1)} %gather_fusion.28), kind=kOutput, calls=%fused_computation.71 | convolution fusion | flops 50331648 | bytes 1966080 | tf_op jit(solution)/shard_map/cnb,nbd->cnd/dot_general | solution.py:23
  113.9 1.6 %fusion.60 = f32[24,64,128]{2,1,0:T(8,128)S(1)} fusion(bf16[24,5,128,128]{3,2,1,0:T(8,128)(2,1)} %param.6, bf16[24,64,128]{2,1,0:T(8,128)(2,1)} %gather_fusion.27), kind=kOutput, calls=%fused_computation.95 | convolution fusion | flops 50331648 | bytes 1966080 | tf_op jit(solution)/shard_map/cnb,nbd->cnd/dot_general | solution.py:23
  121.9 23.9 %reduce-scatter.2.cloned.1.call-done = f32[2,8,24,128]{3,1,0,2:T(8,128)} async-done(((f32[2,32,24,128]{3,1,0,2:T(8,128)}), f32[2,8,24,128]{3,1,0,2:T(8,128)}) %reduce-scatter.2.cloned.1.call-update) | async-done | bytes 196624 | tf_op jit(solution)/shard_map/reduce_scatter | solution.py:108
  145.8 1.7 %copy.94 = f32[2,8,24,128]{3,2,1,0:T(8,128)} copy(f32[2,8,24,128]{3,1,0,2:T(8,128)} %reduce-scatter.2.cloned.1.call-done) | data formatting | bytes 393216 | tf_op jit(solution)/shard_map/reduce_scatter | solution.py:108
  (174 shorter events, 49.0 us)
Async XLA Ops:
  6.5 44.4 %copy-start = (bf16[1,2,24,128,128]{4,3,2,1,0:T(8,128)(2,1)S(1)}, bf16[1,2,24,128,128]{4,3,2,1,0:T(8,128)(2,1)}, u32[]{:S(2)}) copy-start(bf16[1,2,24,128,128]{4,3,2,1,0:T(8,128)(2,1)} %param.8) | copy-start | bytes 4718596
  6.5 139.3 %reduce-scatter.2.cloned.1.call-start = ((), (), s32[]{:S(2)}) async-start(), calls=%async_computation.1 | async-start | bytes 983040 | tf_op jit(solution)/shard_map/reduce_scatter | solution.py:108
  8.2 10.5 %collective-permute-start.4 = (s32[6]{0:T(128)S(1)}, s32[6]{0:T(128)S(1)}, u32[]{:S(2)}, u32[]{:S(2)}) collective-permute-start(s32[6]{0:T(128)S(1)} %get-tuple-element.12), channel_id=1, source_target_pairs={{0,1},{1,2},{2,3},{3,4},{4,5},{5,6},{6,7},{7,0},{8,9},{9,10},{10,1... | collective-permute-start | bytes 80 | tf_op jit(solution)/shard_map/ppermute | solution.py:16
  11.2 7.5 %collective-permute-start.2 = (s32[6]{0:T(128)S(1)}, s32[6]{0:T(128)S(1)}, u32[]{:S(2)}, u32[]{:S(2)}) collective-permute-start(s32[6]{0:T(128)S(1)} %get-tuple-element.11), channel_id=1, source_target_pairs={{0,7},{1,0},{2,1},{3,2},{4,3},{5,4},{6,5},{7,6},{8,15},{9,8},{10,9... | collective-permute-start | bytes 80 | tf_op jit(solution)/shard_map/ppermute | solution.py:16
  14.3 6.8 %collective-permute-start = (s32[6]{0:T(128)S(1)}, s32[6]{0:T(128)S(1)}, u32[]{:S(2)}, u32[]{:S(2)}) collective-permute-start(s32[6]{0:T(128)S(1)} %get-tuple-element.14), channel_id=1, source_target_pairs={{0,6},{1,7},{2,0},{3,1},{4,2},{5,3},{6,4},{7,5},{8,14},{9,15},{10,... | collective-permute-start | bytes 80 | tf_op jit(solution)/shard_map/ppermute | solution.py:16
  16.2 15.0 %collective-permute-start.8 = (s32[6]{0:T(128)S(1)}, s32[6]{0:T(128)S(1)}, u32[]{:S(2)}, u32[]{:S(2)}) collective-permute-start(s32[6]{0:T(128)S(1)} %get-tuple-element.10), channel_id=1, source_target_pairs={{0,4},{1,5},{2,6},{3,7},{4,0},{5,1},{6,2},{7,3},{8,12},{9,13},{10,... | collective-permute-start | bytes 80 | tf_op jit(solution)/shard_map/ppermute | solution.py:16
  16.2 15.0 %collective-permute-start.6 = (s32[6]{0:T(128)S(1)}, s32[6]{0:T(128)S(1)}, u32[]{:S(2)}, u32[]{:S(2)}) collective-permute-start(s32[6]{0:T(128)S(1)} %get-tuple-element.13), channel_id=1, source_target_pairs={{0,2},{1,3},{2,4},{3,5},{4,6},{5,7},{6,0},{7,1},{8,10},{9,11},{10,... | collective-permute-start | bytes 80 | tf_op jit(solution)/shard_map/ppermute | solution.py:16
  18.6 23.6 %copy-start.23 = (s32[1024]{0:T(1024)}, s32[1024]{0:T(1024)S(1)}, u32[]{:S(2)}) copy-start(s32[1024]{0:T(1024)S(1)} %pad_clamp_fusion.4) | copy-start | bytes 12292
  18.6 23.6 %copy-start.24 = (s32[1024]{0:T(1024)}, s32[1024]{0:T(1024)S(1)}, u32[]{:S(2)}) copy-start(s32[1024]{0:T(1024)S(1)} %get-tuple-element.39) | copy-start | bytes 12292
  18.6 23.6 %copy-start.25 = (s32[1024]{0:T(1024)}, s32[1024]{0:T(1024)S(1)}, u32[]{:S(2)}) copy-start(s32[1024]{0:T(1024)S(1)} %get-tuple-element.38) | copy-start | bytes 12292
  18.7 23.6 %copy-start.26 = (s32[1024]{0:T(1024)}, s32[1024]{0:T(1024)S(1)}, u32[]{:S(2)}) copy-start(s32[1024]{0:T(1024)S(1)} %get-tuple-element.36) | copy-start | bytes 12292
  18.7 27.1 %copy-start.27 = (s32[1024]{0:T(1024)}, s32[1024]{0:T(1024)S(1)}, u32[]{:S(2)}) copy-start(s32[1024]{0:T(1024)S(1)} %get-tuple-element.37) | copy-start | bytes 12292
  20.4 14.3 %collective-permute-start.3 = (bf16[32,6,128]{2,1,0:T(8,128)(2,1)S(1)}, bf16[32,6,128]{2,1,0:T(8,128)(2,1)S(1)}, u32[]{:S(2)}, u32[]{:S(2)}) collective-permute-start(bf16[32,6,128]{2,1,0:T(8,128)(2,1)S(1)} %bitcast.248), channel_id=1, source_target_pairs={{0,1},{1,2},{2,3},{3,4},{4,5},{5,6},{6,7},{7,0},{8,9},{9,10},{10,1... | collective-permute-start | bytes 147464 | tf_op jit(solution)/shard_map/ppermute | solution.py:16
  22.8 12.0 %collective-permute-start.1 = (bf16[32,6,128]{2,1,0:T(8,128)(2,1)S(1)}, bf16[32,6,128]{2,1,0:T(8,128)(2,1)S(1)}, u32[]{:S(2)}, u32[]{:S(2)}) collective-permute-start(bf16[32,6,128]{2,1,0:T(8,128)(2,1)S(1)} %bitcast.250), channel_id=1, source_target_pairs={{0,2},{1,3},{2,4},{3,5},{4,6},{5,7},{6,0},{7,1},{8,10},{9,11},{10,... | collective-permute-start | bytes 147464 | tf_op jit(solution)/shard_map/ppermute | solution.py:16
  27.0 7.8 %collective-permute-start.5 = (bf16[32,6,128]{2,1,0:T(8,128)(2,1)S(1)}, bf16[32,6,128]{2,1,0:T(8,128)(2,1)S(1)}, u32[]{:S(2)}, u32[]{:S(2)}) collective-permute-start(bf16[32,6,128]{2,1,0:T(8,128)(2,1)S(1)} %bitcast.249), channel_id=1, source_target_pairs={{0,7},{1,0},{2,1},{3,2},{4,3},{5,4},{6,5},{7,6},{8,15},{9,8},{10,9... | collective-permute-start | bytes 147464 | tf_op jit(solution)/shard_map/ppermute | solution.py:16
  32.9 4.3 %collective-permute-start.7 = (bf16[32,6,128]{2,1,0:T(8,128)(2,1)S(1)}, bf16[32,6,128]{2,1,0:T(8,128)(2,1)S(1)}, u32[]{:S(2)}, u32[]{:S(2)}) collective-permute-start(bf16[32,6,128]{2,1,0:T(8,128)(2,1)S(1)} %bitcast.252), channel_id=1, source_target_pairs={{0,6},{1,7},{2,0},{3,1},{4,2},{5,3},{6,4},{7,5},{8,14},{9,15},{10,... | collective-permute-start | bytes 147464 | tf_op jit(solution)/shard_map/ppermute | solution.py:16
  34.6 5.2 %collective-permute-start.9 = (bf16[32,6,128]{2,1,0:T(8,128)(2,1)S(1)}, bf16[32,6,128]{2,1,0:T(8,128)(2,1)S(1)}, u32[]{:S(2)}, u32[]{:S(2)}) collective-permute-start(bf16[32,6,128]{2,1,0:T(8,128)(2,1)S(1)} %bitcast.251), channel_id=1, source_target_pairs={{0,4},{1,5},{2,6},{3,7},{4,0},{5,1},{6,2},{7,3},{8,12},{9,13},{10,... | collective-permute-start | bytes 147464 | tf_op jit(solution)/shard_map/ppermute | solution.py:16
  51.3 11.0 %copy-start.8 = (bf16[2,32,24,128]{3,1,0,2:T(8,128)(2,1)}, bf16[2,32,24,128]{3,1,0,2:T(8,128)(2,1)S(1)}, u32[]{:S(2)}) copy-start(bf16[2,32,24,128]{3,1,0,2:T(8,128)(2,1)S(1)} %get-tuple-element.34) | copy-start | bytes 1179652
  55.5 7.8 %collective-permute-start.10 = (bf16[64,6,128]{2,0,1:T(8,128)(2,1)}, bf16[64,6,128]{2,0,1:T(8,128)(2,1)S(1)}, u32[]{:S(2)}, u32[]{:S(2)}) collective-permute-start(bf16[64,6,128]{2,0,1:T(8,128)(2,1)} %bitcast.21), channel_id=1, source_target_pairs={{0,2},{1,3},{2,4},{3,5},{4,6},{5,7},{6,0},{7,1},{8,10},{9,11},{10,... | collective-permute-start | bytes 294920 | tf_op jit(solution)/shard_map/ppermute | solution.py:16
  57.6 7.7 %collective-permute-start.11 = (bf16[64,6,128]{2,0,1:T(8,128)(2,1)}, bf16[64,6,128]{2,0,1:T(8,128)(2,1)S(1)}, u32[]{:S(2)}, u32[]{:S(2)}) collective-permute-start(bf16[64,6,128]{2,0,1:T(8,128)(2,1)} %bitcast.22), channel_id=1, source_target_pairs={{0,1},{1,2},{2,3},{3,4},{4,5},{5,6},{6,7},{7,0},{8,9},{9,10},{10,1... | collective-permute-start | bytes 294920 | tf_op jit(solution)/shard_map/ppermute | solution.py:16
  57.6 7.7 %collective-permute-start.12 = (bf16[64,6,128]{2,0,1:T(8,128)(2,1)S(1)}, bf16[64,6,128]{2,0,1:T(8,128)(2,1)S(1)}, u32[]{:S(2)}, u32[]{:S(2)}) collective-permute-start(bf16[64,6,128]{2,0,1:T(8,128)(2,1)S(1)} %bitcast.247), channel_id=1, source_target_pairs={{0,7},{1,0},{2,1},{3,2},{4,3},{5,4},{6,5},{7,6},{8,15},{9,8},{10,9... | collective-permute-start | bytes 294920 | tf_op jit(solution)/shard_map/ppermute | solution.py:16
  62.3 5.7 %collective-permute-start.13 = (bf16[64,6,128]{2,0,1:T(8,128)(2,1)S(1)}, bf16[64,6,128]{2,0,1:T(8,128)(2,1)S(1)}, u32[]{:S(2)}, u32[]{:S(2)}) collective-permute-start(bf16[64,6,128]{2,0,1:T(8,128)(2,1)S(1)} %bitcast.245), channel_id=1, source_target_pairs={{0,6},{1,7},{2,0},{3,1},{4,2},{5,3},{6,4},{7,5},{8,14},{9,15},{10,... | collective-permute-start | bytes 294920 | tf_op jit(solution)/shard_map/ppermute | solution.py:16
  62.3 5.7 %collective-permute-start.14 = (bf16[64,6,128]{2,0,1:T(8,128)(2,1)S(1)}, bf16[64,6,128]{2,0,1:T(8,128)(2,1)S(1)}, u32[]{:S(2)}, u32[]{:S(2)}) collective-permute-start(bf16[64,6,128]{2,0,1:T(8,128)(2,1)S(1)} %bitcast.243), channel_id=1, source_target_pairs={{0,4},{1,5},{2,6},{3,7},{4,0},{5,1},{6,2},{7,3},{8,12},{9,13},{10,... | collective-permute-start | bytes 294920 | tf_op jit(solution)/shard_map/ppermute | solution.py:16
  75.5 6.6 %copy-start.20 = (bf16[24,64,128]{2,1,0:T(8,128)(2,1)S(1)}, bf16[24,64,128]{2,1,0:T(8,128)(2,1)}, u32[]{:S(2)}) copy-start(bf16[24,64,128]{2,1,0:T(8,128)(2,1)} %gather_fusion.16) | copy-start | bytes 1179652
  86.2 11.2 %copy-start.9 = (bf16[2,32,24,128]{3,1,0,2:T(8,128)(2,1)}, bf16[2,32,24,128]{3,1,0,2:T(8,128)(2,1)S(1)}, u32[]{:S(2)}) copy-start(bf16[2,32,24,128]{3,1,0,2:T(8,128)(2,1)S(1)} %fusion.135) | copy-start | bytes 1179652
  90.5 8.4 %collective-permute-start.15 = (bf16[64,6,128]{2,0,1:T(8,128)(2,1)}, bf16[64,6,128]{2,0,1:T(8,128)(2,1)S(1)}, u32[]{:S(2)}, u32[]{:S(2)}) collective-permute-start(bf16[64,6,128]{2,0,1:T(8,128)(2,1)} %bitcast.47), channel_id=1, source_target_pairs={{0,2},{1,3},{2,4},{3,5},{4,6},{5,7},{6,0},{7,1},{8,10},{9,11},{10,... | collective-permute-start | bytes 294920 | tf_op jit(solution)/shard_map/ppermute | solution.py:16
  92.4 7.6 %collective-permute-start.16 = (bf16[64,6,128]{2,0,1:T(8,128)(2,1)}, bf16[64,6,128]{2,0,1:T(8,128)(2,1)S(1)}, u32[]{:S(2)}, u32[]{:S(2)}) collective-permute-start(bf16[64,6,128]{2,0,1:T(8,128)(2,1)} %bitcast.48), channel_id=1, source_target_pairs={{0,1},{1,2},{2,3},{3,4},{4,5},{5,6},{6,7},{7,0},{8,9},{9,10},{10,1... | collective-permute-start | bytes 294920 | tf_op jit(solution)/shard_map/ppermute | solution.py:16
  92.4 7.6 %collective-permute-start.17 = (bf16[64,6,128]{2,0,1:T(8,128)(2,1)S(1)}, bf16[64,6,128]{2,0,1:T(8,128)(2,1)S(1)}, u32[]{:S(2)}, u32[]{:S(2)}) collective-permute-start(bf16[64,6,128]{2,0,1:T(8,128)(2,1)S(1)} %bitcast.246), channel_id=1, source_target_pairs={{0,7},{1,0},{2,1},{3,2},{4,3},{5,4},{6,5},{7,6},{8,15},{9,8},{10,9... | collective-permute-start | bytes 294920 | tf_op jit(solution)/shard_map/ppermute | solution.py:16
  97.1 4.6 %collective-permute-start.18 = (bf16[64,6,128]{2,0,1:T(8,128)(2,1)S(1)}, bf16[64,6,128]{2,0,1:T(8,128)(2,1)S(1)}, u32[]{:S(2)}, u32[]{:S(2)}) collective-permute-start(bf16[64,6,128]{2,0,1:T(8,128)(2,1)S(1)} %bitcast.244), channel_id=1, source_target_pairs={{0,6},{1,7},{2,0},{3,1},{4,2},{5,3},{6,4},{7,5},{8,14},{9,15},{10,... | collective-permute-start | bytes 294920 | tf_op jit(solution)/shard_map/ppermute | solution.py:16
  97.4 5.5 %collective-permute-start.19 = (bf16[64,6,128]{2,0,1:T(8,128)(2,1)S(1)}, bf16[64,6,128]{2,0,1:T(8,128)(2,1)S(1)}, u32[]{:S(2)}, u32[]{:S(2)}) collective-permute-start(bf16[64,6,128]{2,0,1:T(8,128)(2,1)S(1)} %bitcast.242), channel_id=1, source_target_pairs={{0,4},{1,5},{2,6},{3,7},{4,0},{5,1},{6,2},{7,3},{8,12},{9,13},{10,... | collective-permute-start | bytes 294920 | tf_op jit(solution)/shard_map/ppermute | solution.py:16
  110.4 6.6 %copy-start.2 = (bf16[24,5,128,128]{3,2,1,0:T(8,128)(2,1)S(1)}, bf16[24,5,128,128]{3,2,1,0:T(8,128)(2,1)}, u32[]{:S(2)}) copy-start(bf16[24,5,128,128]{3,2,1,0:T(8,128)(2,1)} %param.6) | copy-start | bytes 11796484
  110.4 6.6 %copy-start.17 = (bf16[24,64,128]{2,1,0:T(8,128)(2,1)S(1)}, bf16[24,64,128]{2,1,0:T(8,128)(2,1)}, u32[]{:S(2)}) copy-start(bf16[24,64,128]{2,1,0:T(8,128)(2,1)} %gather_fusion.26) | copy-start | bytes 1179652
  (17 other events, 46.2 us)
Sparse Core Ops, SparseCore 0:
  122.0 23.7 reduce-scatter.1
where the time goes:
time: 155 us; the launch traced here: 154 us
  local copies, waits for them, and re-layouts  43.2 us (28%)
  waiting for transfers between devices  37.4 us (24%)
  starting transfers between devices  30.7 us (20%)
  matrix products  25.7 us (17%)
  between operations  14.3 us (9%)
  other arithmetic  3.01 us (2%)
    ppermute x20, starting transfers between devices, from_behind(): lax.ppermute(value, axis, [(i, (i + by) % devices) for i in range(devices)])  30.7 us
    dot_general x25, matrix products, apply_blocks(): jnp.einsum('cnb,nbd->cnd', picked, matrices[:, slot], preferred_element_t...  24.6 us
    reduce_scatter x1, waiting for transfers between devices, per_device(): return lax.psum_scatter(weighted, 'node', scatter_dimension=1, tiled=True)  23.9 us
    gather x15, local copies, waits for them, and re-layouts, apply_blocks(): picked = extended[:, slot_index[:, slot], :]  17.8 us
    gather x15, local copies, waits for them, and re-layouts, fetch_halo(): outgoing = vector[:, asked_for, :]  16.8 us
    ppermute x20, waiting for transfers between devices, from_behind(): lax.ppermute(value, axis, [(i, (i + by) % devices) for i in range(devices)])  13.5 us
    unnamed x72, local copies, waits for them, and re-layouts  6.59 us
  transfers between devices with their start and end apart: 21, of which 8 were waited for; matrix products, arithmetic and copies ran while one was open for 8% of the time, Pallas kernels for 0%

commit v1 on v0

v1 whole, which is shorter than its diff:
```python
import functools
import math

import jax
import jax.numpy as jnp
from jax import lax
from jax.experimental import pallas as pl
from jax.experimental.pallas import tpu as pltpu
from jax.sharding import PartitionSpec as P

SLOTS = 5
HMAX = 6
REACH = 2
SWEEPS = 2
LANES = 2 * REACH + 1
HALO = LANES * HMAX
MESH = pl.DeviceIdType.MESH
ROW_STEP = 4


def lane_offsets(peer_count):
    return list(range(-REACH, 0)) + list(range(1, REACH + 1)) + [peer_count // 2]


def index_tables(neighbours, dev_rows, peer_count):
    my_index = lax.axis_index("rows")
    flat = neighbours.reshape(-1)
    owner = flat // dev_rows
    local = flat - owner * dev_rows
    remote = owner != my_index
    half_cycle = peer_count // 2
    off = (owner - my_index + peer_count) % peer_count
    far = off == half_cycle
    off = jnp.where(off > half_cycle, off - peer_count, off)
    lane = jnp.where(off < 0, off + REACH, off + REACH - 1)
    lane = jnp.where(far, 2 * REACH, lane)
    lane = jnp.where(remote, lane, -1)
    position = jnp.arange(flat.shape[0], dtype=jnp.int32)
    earlier = (lane[None, :] == lane[:, None]) & (position[None, :] < position[:, None])
    rank = jnp.sum(earlier.astype(jnp.int32), axis=1)
    place = jnp.where(remote, lane * HMAX + rank, -1)
    matched = place[None, :] == jnp.arange(HALO, dtype=jnp.int32)[:, None]
    entry = jnp.sum(jnp.where(matched, position[None, :], 0), axis=1)
    wanted = jnp.sum(jnp.where(matched, local[None, :], 0), axis=1)
    own = jnp.where(remote, dev_rows, local)
    arrived = jnp.where(remote, place, HALO)
    table = jnp.concatenate([own, arrived, entry])
    wanted = jnp.pad(wanted.reshape(LANES, 1, HMAX), ((0, 0), (0, 7), (0, 128 - HMAX)))
    return table, wanted


def kernel(
    peer_count,
    node_count,
    table_ref,
    want_ref,
    cols_ref,
    e_ref,
    a_ref,
    p_ref,
    out_ref,
    weights,
    inverse,
    asked_v,
    asked_s,
    send_0,
    send_1,
    send_2,
    halo_0,
    halo_1,
    halo_2,
    vec_1,
    vec_2,
    part_0,
    part,
    prod_0,
    prod,
    rhs,
    iterate,
    share,
    mixed,
    from_core,
    from_y,
    load_sem,
    asked_sem,
    want_send,
    want_recv,
    halo_send,
    halo_recv,
    core_send,
    core_recv,
    y_send,
    y_recv,
):
    dev_rows = rhs.shape[0]
    col_count = rhs.shape[1]
    block = rhs.shape[2]
    entries = dev_rows * SLOTS
    offsets = lane_offsets(peer_count)
    me = lax.axis_index("rows")
    node = lax.axis_index("node")
    y_count = node_count // 2
    my_y = node // 2
    my_core = node % 2
    own_at, arrived_at, entry_at = 0, entries, 2 * entries

    loads = [
        pltpu.make_async_copy(e_ref, weights.at[:, :, 0:block], load_sem.at[0]),
        pltpu.make_async_copy(a_ref, weights.at[:, :, block : 2 * block], load_sem.at[1]),
        pltpu.make_async_copy(p_ref.at[0], inverse.at[:, :, 0:block], load_sem.at[2]),
        pltpu.make_async_copy(p_ref.at[1], inverse.at[:, :, block : 2 * block], load_sem.at[3]),
    ]
    loads[0].start()
    loads[2].start()
    loads[3].start()
    loads[1].start()

    def behind(offset):
        return lax.rem(me + offset + peer_count, peer_count)

    barrier = pltpu.get_barrier_semaphore()
    for offset in offsets:
        pl.semaphore_signal(barrier, inc=1, device_id={"rows": behind(offset)}, device_id_type=MESH)
    for step in range(1, node_count):
        other = lax.rem(node + step, node_count)
        pl.semaphore_signal(barrier, inc=1, device_id={"node": other}, device_id_type=MESH)
    pl.semaphore_wait(barrier, LANES + node_count - 1)

    pending = []
    for lane, offset in enumerate(offsets):
        copy = pltpu.make_async_remote_copy(
            src_ref=want_ref.at[lane],
            dst_ref=asked_v.at[lane],
            send_sem=want_send.at[lane],
            recv_sem=want_recv.at[lane],
            device_id={"rows": behind(offset)},
            device_id_type=MESH,
        )
        copy.start()
        pending.append(copy)

    vec_1[dev_rows] = jnp.zeros(vec_1.shape[1:], vec_1.dtype)
    vec_2[dev_rows] = jnp.zeros(vec_2.shape[1:], vec_2.dtype)
    prod_0[HALO] = jnp.zeros(prod_0.shape[1:], prod_0.dtype)
    prod[HALO] = jnp.zeros(prod.shape[1:], prod.dtype)

    for copy in pending:
        copy.wait_recv()
    to_scalars = pltpu.make_async_copy(asked_v, asked_s, asked_sem)
    to_scalars.start()
    to_scalars.wait()

    lane_order = [LANES - 1] + list(range(LANES - 1))

    def send_halo(phase, vector, outgoing, halo):
        copies = [None] * LANES
        for lane in lane_order:
            for rank in range(HMAX):
                outgoing[lane * HMAX + rank] = vector[asked_s[lane, 0, rank]]
            here = pl.ds(lane * HMAX, HMAX)
            copy = pltpu.make_async_remote_copy(
                src_ref=outgoing.at[here],
                dst_ref=halo.at[here],
                send_sem=halo_send.at[phase, lane],
                recv_sem=halo_recv.at[phase, lane],
                device_id={"rows": behind(-offsets[lane])},
                device_id_type=MESH,
            )
            copy.start()
            copies[lane] = copy
            pending.append(copy)
        return copies

    def own_products(vector, width, target):
        def rows(step, carry):
            for part_row in range(ROW_STEP):
                row = step * ROW_STEP + part_row
                at = row * SLOTS
                picked = [vector[table_ref[own_at + at + slot]] for slot in range(SLOTS)]
                matrix = weights[pl.ds(at, SLOTS), :, 0:width].reshape(SLOTS * block, width)
                target[row] = jnp.dot(
                    jnp.concatenate(picked, axis=1), matrix, preferred_element_type=jnp.float32
                )
            return carry

        lax.fori_loop(0, dev_rows // ROW_STEP, rows, 0)

    def halo_products(copies, halo, width, target):
        for lane in (1, 2, 0, 3, 4):
            copies[lane].wait_recv()

            def ranks(step, carry):
                for part_rank in range(HMAX // 2):
                    at = lane * HMAX + step * (HMAX // 2) + part_rank
                    matrix = weights[table_ref[entry_at + at], :, 0:width]
                    target[at] = jnp.dot(halo[at], matrix, preferred_element_type=jnp.float32)
                return carry

            lax.fori_loop(0, 2, ranks, 0)

    def all_products(row, target, halo_target):
        summed = target[row]
        for slot in range(1, SLOTS):
            summed = summed + halo_target[table_ref[arrived_at + row * SLOTS + slot]]
        return summed

    node_real = jnp.float32(0.0)
    node_imag = jnp.float32(0.0)
    for index in range(node_count):
        angle = 2.0 * math.pi * (index + 0.5) / node_count
        node_real = jnp.where(node == index, jnp.float32(math.cos(angle)), node_real)
        node_imag = jnp.where(node == index, jnp.float32(math.sin(angle)), node_imag)

    copies = send_halo(0, cols_ref, send_0, halo_0)
    loads[0].wait()
    own_products(cols_ref, block, part_0)
    loads[1].wait()
    halo_products(copies, halo_0, block, prod_0)
    loads[2].wait()
    loads[3].wait()

    def first_rows(step, carry):
        for part_row in range(ROW_STEP):
            row = step * ROW_STEP + part_row
            right = all_products(row, part_0, prod_0)
            rhs[row] = right
            both = jnp.dot(
                right.astype(jnp.bfloat16), inverse[row], preferred_element_type=jnp.float32
            )
            fresh = jnp.concatenate([both[:, 0:block], both[:, block:]], axis=0)
            iterate[row] = fresh
            vec_1[row] = fresh.astype(jnp.bfloat16)
        return carry

    lax.fori_loop(0, dev_rows // ROW_STEP, first_rows, 0)

    chunk = col_count // node_count
    for sweep in range(SWEEPS):
        vector, outgoing, halo = [(vec_1, send_1, halo_1), (vec_2, send_2, halo_2)][sweep]
        copies = send_halo(1 + sweep, vector, outgoing, halo)
        own_products(vector, 2 * block, part)
        halo_products(copies, halo, 2 * block, prod)

        def sweep_rows(step, carry):
            for part_row in range(ROW_STEP):
                row = step * ROW_STEP + part_row
                both = all_products(row, part, prod)
                e_real, a_real = both[:col_count, :block], both[:col_count, block:]
                e_imag, a_imag = both[col_count:, :block], both[col_count:, block:]
                res_real = rhs[row] - (node_real * e_real - node_imag * e_imag - a_real)
                res_imag = -(node_real * e_imag + node_imag * e_real - a_imag)
                residual = jnp.concatenate([res_real, res_imag], axis=0).astype(jnp.bfloat16)
                moved = jnp.dot(residual, inverse[row], preferred_element_type=jnp.float32)
                real = iterate[row, 0:col_count] + (
                    moved[:col_count, :block] - moved[col_count:, block:]
                )
                imag = iterate[row, col_count : 2 * col_count] + (
                    moved[:col_count, block:] + moved[col_count:, :block]
                )
                if sweep < SWEEPS - 1:
                    iterate[row, 0:col_count] = real
                    iterate[row, col_count : 2 * col_count] = imag
                    vec_2[row] = jnp.concatenate([real, imag], axis=0).astype(jnp.bfloat16)
                else:
                    out_real = (node_real * real - node_imag * imag) / node_count
                    out_imag = (node_real * imag + node_imag * real) / node_count
                    for y in range(y_count):
                        for core in range(2):
                            at = (2 * y + core) * chunk
                            share[core, y, row, 0:chunk] = out_real[at : at + chunk]
                            share[core, y, row, chunk : 2 * chunk] = out_imag[at : at + chunk]
            return carry

        lax.fori_loop(0, dev_rows // ROW_STEP, sweep_rows, 0)

    to_core = pltpu.make_async_remote_copy(
        src_ref=share.at[1 - my_core],
        dst_ref=from_core,
        send_sem=core_send,
        recv_sem=core_recv,
        device_id={"node": 2 * my_y + (1 - my_core)},
        device_id_type=MESH,
    )
    to_core.start()
    pending.append(to_core)
    to_core.wait_recv()
    arrivals = []
    for step in range(1, y_count):
        other = lax.rem(my_y + step, y_count)
        mixed[step] = share[my_core, other] + from_core[other]
        copy = pltpu.make_async_remote_copy(
            src_ref=mixed.at[step],
            dst_ref=from_y.at[step - 1],
            send_sem=y_send.at[step - 1],
            recv_sem=y_recv.at[step - 1],
            device_id={"node": 2 * other + my_core},
            device_id_type=MESH,
        )
        copy.start()
        arrivals.append(copy)
        pending.append(copy)
    mixed[0] = share[my_core, my_y] + from_core[my_y]
    for copy in arrivals:
        copy.wait_recv()
    total = mixed[0]
    for step in range(1, y_count):
        total = total + from_y[step - 1]
    out_ref[...] = total
    for copy in pending:
        copy.wait_send()


def per_device(peer_count, node_count, columns, pencil_e, pencil_a, precond, neighbours):
    dev_rows, _, block, _ = pencil_e.shape
    col_count = columns.shape[0]
    pairs = 2 * col_count
    chunk = col_count // node_count
    y_count = node_count // 2
    entries = dev_rows * SLOTS
    table, wanted = index_tables(neighbours, dev_rows, peer_count)
    turned = jnp.pad(columns.transpose(1, 0, 2), ((0, 1), (0, 0), (0, 0)))
    half, full = jnp.bfloat16, jnp.float32
    vmem = pl.BlockSpec(memory_space=pltpu.VMEM)
    anywhere = pl.BlockSpec(memory_space=pl.ANY)
    dma = pltpu.SemaphoreType.DMA
    scratch = [
        pltpu.VMEM((entries, block, 2 * block), half),
        pltpu.VMEM((dev_rows, block, 2 * block), half),
        pltpu.VMEM((LANES, 8, 128), jnp.int32),
        pltpu.SMEM((LANES, 8, 128), jnp.int32),
        pltpu.VMEM((HALO, col_count, block), half),
        pltpu.VMEM((HALO, pairs, block), half),
        pltpu.VMEM((HALO, pairs, block), half),
        pltpu.VMEM((HALO, col_count, block), half),
        pltpu.VMEM((HALO, pairs, block), half),
        pltpu.VMEM((HALO, pairs, block), half),
        pltpu.VMEM((dev_rows + 1, pairs, block), half),
        pltpu.VMEM((dev_rows + 1, pairs, block), half),
        pltpu.VMEM((dev_rows, col_count, block), full),
        pltpu.VMEM((dev_rows, pairs, 2 * block), full),
        pltpu.VMEM((HALO + 1, col_count, block), full),
        pltpu.VMEM((HALO + 1, pairs, 2 * block), full),
        pltpu.VMEM((dev_rows, col_count, block), full),
        pltpu.VMEM((dev_rows, pairs, block), full),
        pltpu.VMEM((2, y_count, dev_rows, 2 * chunk, block), full),
        pltpu.VMEM((y_count, dev_rows, 2 * chunk, block), full),
        pltpu.VMEM((y_count, dev_rows, 2 * chunk, block), full),
        pltpu.VMEM((max(y_count - 1, 1), dev_rows, 2 * chunk, block), full),
        dma((4,)),
        dma,
        dma((LANES,)),
        dma((LANES,)),
        dma((1 + SWEEPS, LANES)),
        dma((1 + SWEEPS, LANES)),
        dma,
        dma,
        dma((max(y_count - 1, 1),)),
        dma((max(y_count - 1, 1),)),
    ]
    summed = pl.pallas_call(
        functools.partial(kernel, peer_count, node_count),
        out_shape=jax.ShapeDtypeStruct((dev_rows, 2 * chunk, block), full),
        in_specs=[
            pl.BlockSpec(memory_space=pltpu.SMEM),
            vmem,
            vmem,
            anywhere,
            anywhere,
            anywhere,
        ],
        out_specs=vmem,
        scratch_shapes=scratch,
        compiler_params=pltpu.CompilerParams(
            collective_id=0, has_side_effects=True, vmem_limit_bytes=60 * 1024 * 1024
        ),
    )(
        table,
        wanted,
        turned,
        pencil_e.reshape(entries, block, block),
        pencil_a.reshape(entries, block, block),
        precond.reshape(2, dev_rows, block, block),
    )
    return summed.reshape(dev_rows, 2, chunk, block).transpose(1, 2, 0, 3)


def solution(mesh):
    placed = (
        P(None, "rows", None),
        P("rows", None, None, None),
        P("rows", None, None, None),
        P("node", None, "rows", None, None),
        P("rows", None),
    )
    return jax.shard_map(
        functools.partial(per_device, mesh.shape["rows"], mesh.shape["node"]),
        mesh=mesh,
        in_specs=placed,
        out_specs=P(None, "node", "rows", None),
        check_vma=False,
    )
```

time: 155 us -> 57.6 us (0.37)
  Pallas kernels: 0 us -> 51.5 us
  local copies, waits for them, and re-layouts: 43.2 us -> 4.87 us
  waiting for transfers between devices: 37.4 us -> 0 us
  starting transfers between devices: 30.7 us -> 0 us
  matrix products: 25.7 us -> 0 us
  between operations: 14.3 us -> 0.04 us
  other arithmetic: 3.01 us -> 0.98 us
    pallas_call x0 -> x1, Pallas kernels: none -> 51.5 us  [per_device(): pl.pallas_call(functools.partial(kernel, peer_count, node_count), out_sha...]
    gather x30 -> x0, local copies, waits for them, and re-layouts: 34.6 us -> none  [the longest x15 17.8 us: apply_blocks(): picked = extended[:, slot_index[:, slot], :]]
    ppermute x20 -> x0, starting transfers between devices: 30.7 us -> none  [from_behind(): lax.ppermute(value, axis, [(i, (i + by) % devices) for i in range(devices)])]
    dot_general x28 -> x0, matrix products: 25.7 us -> none  [the longest x25 24.6 us: apply_blocks(): jnp.einsum('cnb,nbd->cnd', picked, matrices[:, slot], preferred_element_t...]
    reduce_scatter x1 -> x0, waiting for transfers between devices: 23.9 us -> none  [per_device(): return lax.psum_scatter(weighted, 'node', scatter_dimension=1, tiled=True)]
    ppermute x20 -> x0, waiting for transfers between devices: 13.5 us -> none  [from_behind(): lax.ppermute(value, axis, [(i, (i + by) % devices) for i in range(devices)])]
    unnamed x72 -> x2, local copies, waits for them, and re-layouts: 6.59 us -> 1.72 us
    reshape x1 -> x3, local copies, waits for them, and re-layouts: 0.09 us -> 1.85 us  [the longest x1 1.67 us: per_device(): return summed.reshape(dev_rows, 2, chunk, block).transpose(1, 2, 0, 3)]
  transfers between devices with their start and end apart: 21 -> 0, of which waited for: 8 -> 0; matrix products, arithmetic and copies ran while one was open for 8% -> 0% of each run, Pallas kernels for 0% -> 0%
where the time goes in v1:
time: 57.6 us; the launch traced here: 57.3 us
  Pallas kernels  51.5 us (89%)
  local copies, waits for them, and re-layouts  4.87 us (8%)
  other arithmetic  0.98 us (2%)
    pallas_call x1, Pallas kernels, per_device(): pl.pallas_call(functools.partial(kernel, peer_count, node_count), out_sha...  51.5 us
    unnamed x2, local copies, waits for them, and re-layouts  1.72 us
    reshape x1, local copies, waits for them, and re-layouts, per_device(): return summed.reshape(dev_rows, 2, chunk, block).transpose(1, 2, 0, 3)  1.67 us

profile of v1, /device:TPU:0, one launch (start us, length us, event | category | flops | bytes accessed | tf_op | source)
XLA Modules:
  0.0 57.3 jit_solution(15758606715739617642)
XLA Ops:
  0.0 0.8 %copy.14 = s32[24,5]{1,0:T(8,128)S(1)} copy(s32[24,5]{0,1:T(8,128)} %param.9) | data formatting | bytes 960 | tf_op args[4]
  0.8 0.1 reshape.126
  0.9 0.2 convert_reduce_fusion
  1.1 0.1 select_reduce_fusion
  1.2 0.6 %pad_add_fusion.table_ref = s32[270]{0:T(512)} fusion(s32[30]{0:T(128)S(1)} %get-tuple-element.6, s32[120]{0:T(128)S(1)} %get-tuple-element.10, s32[120]{0:T(128)S(1)} %get-tuple-element.7), kind=kLoop, calls=%fused_computation.11 | loop fusion | flops 540 | bytes 2160 | tf_op jit(solution)/shard_map/concatenate | solution.py:47
  1.9 0.1 reshape.132
  2.0 0.6 %pad.8.want_ref = s32[5,8,128]{2,1,0:T(8,128)} pad(s32[5,1,6]{2,1,0:T(1,128)S(1)} %reshape.132, s32[]{:T(128)} %constant.45.clone.1), padding=0_0x0_7x0_122 | pad | bytes 20604 | tf_op jit(solution)/shard_map/jit(_pad)/pad | solution.py:48
  2.6 1.0 %copy.21 = bf16[32,24,128]{2,0,1:T(8,128)(2,1)S(1)} copy(bf16[32,24,128]{2,1,0:T(8,128)(2,1)} %param.5) | data formatting | bytes 393216 | tf_op args[0]
  3.5 0.7 %pad.9.cols_ref = bf16[25,32,128]{2,1,0:T(8,128)(2,1)} pad(bf16[24,32,128]{2,1,0:T(8,128)(2,1)S(1)} %bitcast.13, bf16[]{:T(256)} %constant.55.clone.1), padding=0_1x0_0x0_0 | pad | bytes 401410 | tf_op jit(solution)/shard_map/jit(_pad)/pad | solution.py:321
  4.2 51.5 %shard_map.55 = f32[24,16,128]{2,1,0:T(8,128)} custom-call(s32[270]{0:T(512)} %pad_add_fusion.table_ref, s32[5,8,128]{2,1,0:T(8,128)} %pad.8.want_ref, bf16[25,32,128]{2,1,0:T(8,128)(2,1)} %pad.9.cols_ref, bf16[120,128,128]{2,1,0:T(8,128)(2,1)} %bitcast.10, bf16[120,128,128]{2,1,0:T(8,128)(2,1)} %bitcast.11, bf16[2,24,128,128]{3,2,1,0:T(8,128)(2,1)} %bitcast.12), custom_call_target="tpu_custom_call" | custom-call | tf_op jit(solution)/shard_map/pallas_call | solution.py:360
  55.7 1.7 %copy.20 = f32[24,2,8,128]{3,0,2,1:T(8,128)} copy(f32[24,2,8,128]{3,2,1,0:T(8,128)} %bitcast.14) | data formatting | bytes 393216 | tf_op jit(solution)/shard_map/reshape | solution.py:384
  (3 shorter events, 0.1 us)

commit v2 on v1

v2 whole, which is shorter than its diff:
```python
import functools
import math

import jax
import jax.numpy as jnp
from jax import lax
from jax.experimental import pallas as pl
from jax.experimental.pallas import tpu as pltpu
from jax.sharding import PartitionSpec as P

SLOTS = 5
HMAX = 6
REACH = 2
SWEEPS = 2
LANES = 2 * REACH + 1
HALO = LANES * HMAX
MESH = pl.DeviceIdType.MESH
ROW_STEP = 4


def lane_offsets(peer_count):
    return list(range(-REACH, 0)) + list(range(1, REACH + 1)) + [peer_count // 2]


def index_tables(neighbours, dev_rows, peer_count):
    my_index = lax.axis_index("rows")
    flat = neighbours.reshape(-1)
    owner = flat // dev_rows
    local = flat - owner * dev_rows
    remote = owner != my_index
    half_cycle = peer_count // 2
    off = (owner - my_index + peer_count) % peer_count
    far = off == half_cycle
    off = jnp.where(off > half_cycle, off - peer_count, off)
    lane = jnp.where(off < 0, off + REACH, off + REACH - 1)
    lane = jnp.where(far, 2 * REACH, lane)
    lane = jnp.where(remote, lane, -1)
    position = jnp.arange(flat.shape[0], dtype=jnp.int32)
    earlier = (lane[None, :] == lane[:, None]) & (position[None, :] < position[:, None])
    rank = jnp.sum(earlier.astype(jnp.int32), axis=1)
    place = jnp.where(remote, lane * HMAX + rank, -1)
    matched = place[None, :] == jnp.arange(HALO, dtype=jnp.int32)[:, None]
    entry = jnp.sum(jnp.where(matched, position[None, :], 0), axis=1)
    wanted = jnp.sum(jnp.where(matched, local[None, :], 0), axis=1)
    own = jnp.where(remote, dev_rows, local)
    arrived = jnp.where(remote, place, HALO)
    return own, arrived, entry, wanted.reshape(LANES, 1, HMAX)


def kernel(
    peer_count,
    node_count,
    own_ref,
    arrived_ref,
    entry_ref,
    want_ref,
    cols_ref,
    e_ref,
    a_ref,
    p_ref,
    out_ref,
    weights,
    inverse,
    wide_cols,
    asked_v,
    asked_s,
    vec_0,
    send_0,
    halo_0,
    part_0,
    prod_0,
    rhs,
    vec,
    outgoing,
    halo,
    part,
    prod,
    iterate,
    share,
    from_core,
    mixed,
    to_y,
    from_y,
    load_sem,
    asked_sem,
    want_send,
    want_recv,
    halo_send,
    halo_recv,
    core_send,
    core_recv,
    y_send,
    y_recv,
):
    dev_rows = rhs.shape[0]
    block = rhs.shape[2]
    batches = vec.shape[1]
    width = vec.shape[3] // 2
    chunk = width // 2
    offsets = lane_offsets(peer_count)
    me = lax.axis_index("rows")
    node = lax.axis_index("node")
    my_y = node // 2
    my_core = node % 2

    def batch_y(batch):
        return lax.rem(my_y + 1 + batch, batches)

    load_e = pltpu.make_async_copy(e_ref, weights.at[:, :, 0:block], load_sem.at[0])
    load_a = pltpu.make_async_copy(a_ref, weights.at[:, :, block : 2 * block], load_sem.at[1])
    load_p = [
        pltpu.make_async_copy(
            p_ref.at[index], inverse.at[:, :, index * block : (index + 1) * block], load_sem.at[2 + index]
        )
        for index in range(2)
    ]
    for copy in [load_e] + load_p + [load_a]:
        copy.start()

    def behind(offset):
        return lax.rem(me + offset + peer_count, peer_count)

    barrier = pltpu.get_barrier_semaphore()
    for offset in offsets:
        pl.semaphore_signal(barrier, inc=1, device_id={"rows": behind(offset)}, device_id_type=MESH)
    for step in range(1, node_count):
        other = lax.rem(node + step, node_count)
        pl.semaphore_signal(barrier, inc=1, device_id={"node": other}, device_id_type=MESH)

    wide_cols[...] = cols_ref[...].astype(jnp.float32)
    for row in range(dev_rows):
        for batch in range(batches):
            at = pl.multiple_of(batch_y(batch) * width, width)
            vec_0[row, batch * width : (batch + 1) * width] = wide_cols[pl.ds(at, width), row, :].astype(
                jnp.bfloat16
            )
    vec_0[dev_rows] = jnp.zeros(vec_0.shape[1:], vec_0.dtype)
    prod_0[HALO] = jnp.zeros(prod_0.shape[1:], prod_0.dtype)
    for batch in range(batches):
        prod[batch, HALO] = jnp.zeros(prod.shape[2:], prod.dtype)
        for sweep in range(SWEEPS):
            vec[sweep, batch, dev_rows] = jnp.zeros(vec.shape[3:], vec.dtype)

    pl.semaphore_wait(barrier, LANES + node_count - 1)

    pending = []
    for lane, offset in enumerate(offsets):
        copy = pltpu.make_async_remote_copy(
            src_ref=want_ref.at[lane],
            dst_ref=asked_v.at[lane],
            send_sem=want_send.at[lane],
            recv_sem=want_recv.at[lane],
            device_id={"rows": behind(offset)},
            device_id_type=MESH,
        )
        copy.start()
        pending.append(copy)
    for copy in pending:
        copy.wait_recv()
    to_scalars = pltpu.make_async_copy(asked_v, asked_s, asked_sem)
    to_scalars.start()
    to_scalars.wait()

    def send_halo(phase, source, leaving, arriving):
        copies = [None] * LANES
        for lane in (4, 0, 3, 1, 2):
            for rank in range(HMAX):
                leaving[lane * HMAX + rank] = source[asked_s[lane, 0, rank]]
            here = pl.ds(lane * HMAX, HMAX)
            copy = pltpu.make_async_remote_copy(
                src_ref=leaving.at[here],
                dst_ref=arriving.at[here],
                send_sem=halo_send.at[phase, lane],
                recv_sem=halo_recv.at[phase, lane],
                device_id={"rows": behind(-offsets[lane])},
                device_id_type=MESH,
            )
            copy.start()
            copies[lane] = copy
            pending.append(copy)
        return copies

    def row_loop(body):
        def step_rows(step, carry):
            for inner in range(ROW_STEP):
                body(step * ROW_STEP + inner)
            return carry

        lax.fori_loop(0, dev_rows // ROW_STEP, step_rows, 0)

    def own_products(source, columns, target):
        def one_row(row):
            at = row * SLOTS
            picked = [source[own_ref[at + slot]] for slot in range(SLOTS)]
            matrix = weights[pl.ds(at, SLOTS), :, 0:columns].reshape(SLOTS * block, columns)
            target[row] = jnp.dot(
                jnp.concatenate(picked, axis=1), matrix, preferred_element_type=jnp.float32
            )

        row_loop(one_row)

    def halo_products(copies, arriving, columns, target):
        for lane in (1, 2, 0, 3, 4):
            copies[lane].wait_recv()

            def some_ranks(step, carry):
                for inner in range(HMAX // 2):
                    at = lane * HMAX + step * (HMAX // 2) + inner
                    matrix = weights[entry_ref[at], :, 0:columns]
                    target[at] = jnp.dot(arriving[at], matrix, preferred_element_type=jnp.float32)
                return carry

            lax.fori_loop(0, 2, some_ranks, 0)

    def all_products(row, target, halo_target):
        summed = target[row]
        for slot in range(1, SLOTS):
            summed = summed + halo_target[arrived_ref[row * SLOTS + slot]]
        return summed

    node_real = jnp.float32(0.0)
    node_imag = jnp.float32(0.0)
    for index in range(node_count):
        angle = 2.0 * math.pi * (index + 0.5) / node_count
        node_real = jnp.where(node == index, jnp.float32(math.cos(angle)), node_real)
        node_imag = jnp.where(node == index, jnp.float32(math.sin(angle)), node_imag)

    copies = send_halo(0, vec_0, send_0, halo_0)
    load_e.wait()
    own_products(vec_0, block, part_0)
    load_a.wait()
    halo_products(copies, halo_0, block, prod_0)
    for copy in load_p:
        copy.wait()

    def right_rows(row):
        rhs[row] = all_products(row, part_0, prod_0)

    row_loop(right_rows)

    def phase_of(sweep, batch):
        return 1 + sweep * batches + batch

    flights = {}
    for batch in range(batches):

        def first_rows(row, batch=batch):
            right = rhs[row, batch * width : (batch + 1) * width]
            both = jnp.dot(
                right.astype(jnp.bfloat16), inverse[row], preferred_element_type=jnp.float32
            )
            fresh = jnp.concatenate([both[:, 0:block], both[:, block:]], axis=0)
            iterate[batch, row] = fresh
            vec[0, batch, row] = fresh.astype(jnp.bfloat16)

        row_loop(first_rows)
        flights[0, batch] = send_halo(
            phase_of(0, batch), vec.at[0, batch], outgoing.at[0, batch], halo.at[0, batch]
        )

    core_copies = []
    y_copies = []

    def finish_core(batch):
        core_copies[batch].wait_recv()
        mixed[batch] = share[batch, my_core] + from_core[batch]
        if batch < batches - 1:
            to_y[batch] = mixed[batch].astype(to_y.dtype)
            copy = pltpu.make_async_remote_copy(
                src_ref=to_y.at[batch],
                dst_ref=from_y.at[batch],
                send_sem=y_send.at[batch],
                recv_sem=y_recv.at[batch],
                device_id={"node": 2 * batch_y(batch) + my_core},
                device_id_type=MESH,
            )
            copy.start()
            y_copies.append(copy)
            pending.append(copy)

    for sweep in range(SWEEPS):
        for batch in range(batches):
            source, arriving = vec.at[sweep, batch], halo.at[sweep, batch]
            target, halo_target = part.at[batch], prod.at[batch]
            own_products(source, 2 * block, target)
            if sweep == SWEEPS - 1 and batch > 0:
                finish_core(batch - 1)
            halo_products(flights[sweep, batch], arriving, 2 * block, halo_target)

            def sweep_rows(row, sweep=sweep, batch=batch, target=target, halo_target=halo_target):
                both = all_products(row, target, halo_target)
                e_real, a_real = both[:width, :block], both[:width, block:]
                e_imag, a_imag = both[width:, :block], both[width:, block:]
                right = rhs[row, batch * width : (batch + 1) * width]
                res_real = right - (node_real * e_real - node_imag * e_imag - a_real)
                res_imag = -(node_real * e_imag + node_imag * e_real - a_imag)
                residual = jnp.concatenate([res_real, res_imag], axis=0).astype(jnp.bfloat16)
                moved = jnp.dot(residual, inverse[row], preferred_element_type=jnp.float32)
                real = iterate[batch, row, 0:width] + (
                    moved[:width, :block] - moved[width:, block:]
                )
                imag = iterate[batch, row, width : 2 * width] + (
                    moved[:width, block:] + moved[width:, :block]
                )
                if sweep < SWEEPS - 1:
                    iterate[batch, row, 0:width] = real
                    iterate[batch, row, width : 2 * width] = imag
                    vec[sweep + 1, batch, row] = jnp.concatenate([real, imag], axis=0).astype(
                        jnp.bfloat16
                    )
                else:
                    out_real = (node_real * real - node_imag * imag) / node_count
                    out_imag = (node_real * imag + node_imag * real) / node_count
                    for core in range(2):
                        at = core * chunk
                        share[batch, core, row, 0:chunk] = out_real[at : at + chunk]
                        share[batch, core, row, chunk : 2 * chunk] = out_imag[at : at + chunk]

            row_loop(sweep_rows)
            if sweep < SWEEPS - 1:
                flights[sweep + 1, batch] = send_halo(
                    phase_of(sweep + 1, batch),
                    vec.at[sweep + 1, batch],
                    outgoing.at[sweep + 1, batch],
                    halo.at[sweep + 1, batch],
                )
            else:
                copy = pltpu.make_async_remote_copy(
                    src_ref=share.at[batch, 1 - my_core],
                    dst_ref=from_core.at[batch],
                    send_sem=core_send.at[batch],
                    recv_sem=core_recv.at[batch],
                    device_id={"node": 2 * my_y + (1 - my_core)},
                    device_id_type=MESH,
                )
                copy.start()
                core_copies.append(copy)
                pending.append(copy)

    finish_core(batches - 1)
    for copy in y_copies:
        copy.wait_recv()
    for row in range(dev_rows):
        total = mixed[batches - 1, row]
        for batch in range(batches - 1):
            total = total + from_y[batch, row].astype(jnp.float32)
        out_ref[:, row, :] = total
    for copy in pending:
        copy.wait_send()


def per_device(peer_count, node_count, columns, pencil_e, pencil_a, precond, neighbours):
    dev_rows, _, block, _ = pencil_e.shape
    col_count = columns.shape[0]
    batches = node_count // 2
    width = col_count // batches
    chunk = width // 2
    entries = dev_rows * SLOTS
    tables = index_tables(neighbours, dev_rows, peer_count)
    half, full = jnp.bfloat16, jnp.float32
    smem = pl.BlockSpec(memory_space=pltpu.SMEM)
    vmem = pl.BlockSpec(memory_space=pltpu.VMEM)
    anywhere = pl.BlockSpec(memory_space=pl.ANY)
    dma = pltpu.SemaphoreType.DMA
    crossings = max(batches - 1, 1)
    scratch = [
        pltpu.VMEM((entries, block, 2 * block), half),
        pltpu.VMEM((dev_rows, block, 2 * block), half),
        pltpu.VMEM((col_count, dev_rows, block), full),
        pltpu.VMEM((LANES, 1, HMAX), jnp.int32),
        pltpu.SMEM((LANES, 1, HMAX), jnp.int32),
        pltpu.VMEM((dev_rows + 1, col_count, block), half),
        pltpu.VMEM((HALO, col_count, block), half),
        pltpu.VMEM((HALO, col_count, block), half),
        pltpu.VMEM((dev_rows, col_count, block), full),
        pltpu.VMEM((HALO + 1, col_count, block), full),
        pltpu.VMEM((dev_rows, col_count, block), full),
        pltpu.VMEM((SWEEPS, batches, dev_rows + 1, 2 * width, block), half),
        pltpu.VMEM((SWEEPS, batches, HALO, 2 * width, block), half),
        pltpu.VMEM((SWEEPS, batches, HALO, 2 * width, block), half),
        pltpu.VMEM((batches, dev_rows, 2 * width, 2 * block), full),
        pltpu.VMEM((batches, HALO + 1, 2 * width, 2 * block), full),
        pltpu.VMEM((batches, dev_rows, 2 * width, block), full),
        pltpu.VMEM((batches, 2, dev_rows, 2 * chunk, block), full),
        pltpu.VMEM((batches, dev_rows, 2 * chunk, block), full),
        pltpu.VMEM((batches, dev_rows, 2 * chunk, block), full),
        pltpu.VMEM((crossings, dev_rows, 2 * chunk, block), half),
        pltpu.VMEM((crossings, dev_rows, 2 * chunk, block), half),
        dma((4,)),
        dma,
        dma((LANES,)),
        dma((LANES,)),
        dma((1 + SWEEPS * batches, LANES)),
        dma((1 + SWEEPS * batches, LANES)),
        dma((batches,)),
        dma((batches,)),
        dma((crossings,)),
        dma((crossings,)),
    ]
    summed = pl.pallas_call(
        functools.partial(kernel, peer_count, node_count),
        out_shape=jax.ShapeDtypeStruct((2 * chunk, dev_rows, block), full),
        in_specs=[smem, smem, smem, vmem, vmem, anywhere, anywhere, anywhere],
        out_specs=vmem,
        scratch_shapes=scratch,
        compiler_params=pltpu.CompilerParams(
            collective_id=0, has_side_effects=True, vmem_limit_bytes=60 * 1024 * 1024
        ),
    )(
        *tables,
        columns,
        pencil_e.reshape(entries, block, block),
        pencil_a.reshape(entries, block, block),
        precond.reshape(2, dev_rows, block, block),
    )
    return summed.reshape(2, chunk, dev_rows, block)


def solution(mesh):
    placed = (
        P(None, "rows", None),
        P("rows", None, None, None),
        P("rows", None, None, None),
        P("node", None, "rows", None, None),
        P("rows", None),
    )
    return jax.shard_map(
        functools.partial(per_device, mesh.shape["rows"], mesh.shape["node"]),
        mesh=mesh,
        in_specs=placed,
        out_specs=P(None, "node", "rows", None),
        check_vma=False,
    )
```

time: 57.6 us -> 53.2 us (0.924)
  Pallas kernels: 51.5 us -> 48.4 us
  local copies, waits for them, and re-layouts: 4.87 us -> 3.14 us
    pallas_call x1, Pallas kernels: 51.5 us -> 48.4 us  [per_device(): pl.pallas_call(functools.partial(kernel, peer_count, node_count), out_sha...]
    pad x2 -> x0, local copies, waits for them, and re-layouts: 1.3 us -> none  [the longest x1 0.69 us: per_device(): turned = jnp.pad(columns.transpose(1, 0, 2), ((0, 1), (0, 0), (0, 0)))]
    reshape x2 -> x1, local copies, waits for them, and re-layouts: 1.75 us -> 0.66 us  [index_tables(): return (own, arrived, entry, wanted.reshape(LANES, 1, HMAX))]
    unnamed x2, local copies, waits for them, and re-layouts: 1.72 us -> 2.38 us
    concatenate x1 -> x0, other arithmetic: 0.65 us -> none  [index_tables(): table = jnp.concatenate([own, arrived, entry])]
where the time goes in v2:
time: 53.2 us; the launch traced here: 53 us
  Pallas kernels  48.4 us (91%)
  local copies, waits for them, and re-layouts  3.14 us (6%)
  other arithmetic  1.42 us (3%)
    pallas_call x1, Pallas kernels, per_device(): pl.pallas_call(functools.partial(kernel, peer_count, node_count), out_sha...  48.4 us
    unnamed x2, local copies, waits for them, and re-layouts  2.38 us

profile of v2, /device:TPU:0, one launch (start us, length us, event | category | flops | bytes accessed | tf_op | source)
XLA Modules:
  0.0 53.0 jit_solution(13532173072925476216)
XLA Ops:
  0.0 0.8 %copy.10 = s32[24,5]{1,0:T(8,128)S(1)} copy(s32[24,5]{0,1:T(8,128)} %param.9) | data formatting | bytes 960 | tf_op args[4]
  0.8 0.1 reshape.126
  0.9 0.2 convert_reduce_fusion
  1.1 0.6 %broadcast_select_fusion = (s32[120]{0:T(128)}, s32[120]{0:T(128)S(1)}, s32[120]{0:T(128)}, s32[120]{0:T(128)S(1)}) fusion(s32[120]{0:T(128)S(1)} %get-tuple-element.10, s32[]{:T(128)S(6)} %axis_index.12, s32[120]{0:T(128)S(1)} %convert_reduce_fusion, s32[120]{0:T(128)S(1)} %get-tuple-element.9, s32[120]{0:T(128)S(1)} %reshape.126), kind=kLoop, calls=%fused_computation.17 | loop fusion | flops 960 | bytes 3844 | tf_op jit(solution)/shard_map/jit(_where)/select_n | solution.py:46
  1.7 0.6 %select_reduce_fusion = (s32[30]{0:T(128)S(1)}, s32[30]{0:T(128)}) fusion(s32[120]{0:T(128)S(1)} %get-tuple-element.14, s32[120]{0:T(128)S(1)} %get-tuple-element.8), kind=kLoop, calls=%fused_computation.3 | loop fusion | flops 17940 | bytes 1200 | tf_op jit(solution)/shard_map/reduce_sum | solution.py:44
  2.3 0.7 %reshape.132.want_ref = s32[5,1,6]{2,1,0:T(1,128)} reshape(s32[30]{0:T(128)S(1)} %get-tuple-element.5) | data formatting | bytes 240 | tf_op jit(solution)/shard_map/reshape | solution.py:47
  3.0 48.4 %shard_map.55 = f32[16,24,128]{2,1,0:T(8,128)} custom-call(s32[120]{0:T(128)} %get-tuple-element.13.own_ref, s32[120]{0:T(128)} %get-tuple-element.7.arrived_ref, s32[30]{0:T(128)} %get-tuple-element.6.entry_ref, s32[5,1,6]{2,1,0:T(1,128)} %reshape.132.want_ref, bf16[32,24,128]{2,1,0:T(8,128)(2,1)} %cols_ref.1, bf16[120,128,128]{2,1,0:T(8,128)(2,1)} %bitcast.4, ...), custom_call_target="tpu_custom_call" | custom-call | tf_op jit(solution)/shard_map/pallas_call | solution.py:400
  51.4 1.6 %copy.13 = f32[2,8,24,128]{3,2,1,0:T(8,128)} copy(f32[2,8,24,128]{3,2,1,0:T(8,128)} %bitcast.7) | data formatting | bytes 393216
  (1 shorter events, 0.0 us)

commit v3 on v2

--- a/solution.py
+++ b/solution.py
@@ -15,45 +15,69 @@
 LANES = 2 * REACH + 1
 HALO = LANES * HMAX
 MESH = pl.DeviceIdType.MESH
-ROW_STEP = 4
+ROW_STEP = 8
 
 
 def lane_offsets(peer_count):
     return list(range(-REACH, 0)) + list(range(1, REACH + 1)) + [peer_count // 2]
 
 
-def index_tables(neighbours, dev_rows, peer_count):
-    my_index = lax.axis_index("rows")
-    flat = neighbours.reshape(-1)
-    owner = flat // dev_rows
-    local = flat - owner * dev_rows
-    remote = owner != my_index
-    half_cycle = peer_count // 2
-    off = (owner - my_index + peer_count) % peer_count
-    far = off == half_cycle
-    off = jnp.where(off > half_cycle, off - peer_count, off)
-    lane = jnp.where(off < 0, off + REACH, off + REACH - 1)
-    lane = jnp.where(far, 2 * REACH, lane)
-    lane = jnp.where(remote, lane, -1)
-    position = jnp.arange(flat.shape[0], dtype=jnp.int32)
-    earlier = (lane[None, :] == lane[:, None]) & (position[None, :] < position[:, None])
-    rank = jnp.sum(earlier.astype(jnp.int32), axis=1)
-    place = jnp.where(remote, lane * HMAX + rank, -1)
-    matched = place[None, :] == jnp.arange(HALO, dtype=jnp.int32)[:, None]
-    entry = jnp.sum(jnp.where(matched, position[None, :], 0), axis=1)
-    wanted = jnp.sum(jnp.where(matched, local[None, :], 0), axis=1)
-    own = jnp.where(remote, dev_rows, local)
-    arrived = jnp.where(remote, place, HALO)
-    return own, arrived, entry, wanted.reshape(LANES, 1, HMAX)
+def lane_sum(value):
+    shift = value.shape[1] // 2
+    while shift:
+        value = value + pltpu.roll(value, shift, 1)
+        shift //= 2
+    return value
+
+
+def index_tables(neighbours, dev_rows, me, owners):
+    wide = 128
+    entries = dev_rows * SLOTS
+    position = lax.broadcasted_iota(jnp.int32, (8, wide), 1)
+    sub = lax.broadcasted_iota(jnp.int32, (8, wide), 0)
+    flat = jnp.zeros((8, wide), jnp.int32)
+    slot_of = jnp.zeros((8, wide), jnp.int32)
+    for slot in range(SLOTS):
+        line = jnp.broadcast_to(neighbours[slot : slot + 1, :], (8, wide))
+        flat = flat + (pltpu.roll(line, slot * dev_rows, 1) if slot else line)
+        if slot:
+            slot_of = slot_of + (position >= slot * dev_rows).astype(jnp.int32)
+    row_of = position - slot_of * dev_rows
+    first = jnp.zeros((8, wide), jnp.int32)
+    for lane, owner in enumerate(owners):
+        first = jnp.where(sub == lane, owner * dev_rows, first)
+    inside = (flat >= first) & (flat < first + dev_rows) & (sub < LANES) & (position < entries)
+    count = jnp.where(inside, 1, 0)
+    shift = 1
+    while shift < wide:
+        count = count + jnp.where(position >= shift, pltpu.roll(count, shift, 1), 0)
+        shift *= 2
+    rank = count - 1
+
+    def over_lanes(value):
+        value = jnp.where(inside, value, 0)
+        for step in (4, 2, 1):
+            value = value + pltpu.roll(value, step, 0)
+        return value
+
+    remote = over_lanes(jnp.ones_like(flat)) > 0
+    arrived = jnp.clip(jnp.where(remote, over_lanes(sub * HMAX + rank), HALO), 0, HALO)
+    place = jnp.where(remote, over_lanes(sub * 8 + rank), -1)
+    local = flat - over_lanes(first)
+    own = jnp.clip(jnp.where(remote, dev_rows, flat - me * dev_rows), 0, dev_rows)
+    entry_of = row_of * SLOTS + slot_of
+    entry, wanted = [], []
+    for lane in range(LANES):
+        matched = place == sub + lane * 8
+        entry.append(jnp.clip(lane_sum(jnp.where(matched, entry_of, 0)), 0, entries - 1))
+        wanted.append(jnp.clip(lane_sum(jnp.where(matched, local, 0)), 0, dev_rows - 1))
+    return own, arrived, entry, wanted
 
 
 def kernel(
     peer_count,
     node_count,
-    own_ref,
-    arrived_ref,
-    entry_ref,
-    want_ref,
+    near_ref,
     cols_ref,
     e_ref,
     a_ref,
@@ -62,6 +86,10 @@
     weights,
     inverse,
     wide_cols,
+    near,
+    table_v,
+    table_s,
+    want_v,
     asked_v,
     asked_s,
     vec_0,
@@ -79,9 +107,9 @@
     share,
     from_core,
     mixed,
-    to_y,
     from_y,
     load_sem,
+    table_sem,
     asked_sem,
     want_send,
     want_recv,
@@ -127,6 +155,19 @@
         other = lax.rem(node + step, node_count)
         pl.semaphore_signal(barrier, inc=1, device_id={"node": other}, device_id_type=MESH)
 
+    near[...] = jnp.zeros(near.shape, near.dtype)
+    near[0:SLOTS, 0:dev_rows] = near_ref[...]
+    own, arrived, entry, wanted = index_tables(
+        near[...], dev_rows, me, [behind(offset) for offset in offsets]
+    )
+    for lane in range(LANES):
+        want_v[lane] = wanted[lane]
+        table_v[lane] = entry[lane]
+    table_v[LANES] = own
+    table_v[LANES + 1] = arrived
+    to_table = pltpu.make_async_copy(table_v, table_s, table_sem)
+    to_table.start()
+
     wide_cols[...] = cols_ref[...].astype(jnp.float32)
     for row in range(dev_rows):
         for batch in range(batches):
@@ -146,7 +187,7 @@
     pending = []
     for lane, offset in enumerate(offsets):
         copy = pltpu.make_async_remote_copy(
-            src_ref=want_ref.at[lane],
+            src_ref=want_v.at[lane],
             dst_ref=asked_v.at[lane],
             send_sem=want_send.at[lane],
             recv_sem=want_recv.at[lane],
@@ -160,12 +201,13 @@
     to_scalars = pltpu.make_async_copy(asked_v, asked_s, asked_sem)
     to_scalars.start()
     to_scalars.wait()
+    to_table.wait()
 
     def send_halo(phase, source, leaving, arriving):
         copies = [None] * LANES
         for lane in (4, 0, 3, 1, 2):
             for rank in range(HMAX):
-                leaving[lane * HMAX + rank] = source[asked_s[lane, 0, rank]]
+                leaving[lane * HMAX + rank] = source[asked_s[lane, rank, 0]]
             here = pl.ds(lane * HMAX, HMAX)
             copy = pltpu.make_async_remote_copy(
                 src_ref=leaving.at[here],
@@ -191,7 +233,7 @@
     def own_products(source, columns, target):
         def one_row(row):
             at = row * SLOTS
-            picked = [source[own_ref[at + slot]] for slot in range(SLOTS)]
+            picked = [source[table_s[LANES, 0, slot * dev_rows + row]] for slot in range(SLOTS)]
             matrix = weights[pl.ds(at, SLOTS), :, 0:columns].reshape(SLOTS * block, columns)
             target[row] = jnp.dot(
                 jnp.concatenate(picked, axis=1), matrix, preferred_element_type=jnp.float32
@@ -203,19 +245,15 @@
         for lane in (1, 2, 0, 3, 4):
             copies[lane].wait_recv()
 
-            def some_ranks(step, carry):
-                for inner in range(HMAX // 2):
-                    at = lane * HMAX + step * (HMAX // 2) + inner
-                    matrix = weights[entry_ref[at], :, 0:columns]
-                    target[at] = jnp.dot(arriving[at], matrix, preferred_element_type=jnp.float32)
-                return carry
-
-            lax.fori_loop(0, 2, some_ranks, 0)
+            for rank in range(HMAX):
+                at = lane * HMAX + rank
+                matrix = weights[table_s[lane, rank, 0], :, 0:columns]
+                target[at] = jnp.dot(arriving[at], matrix, preferred_element_type=jnp.float32)
 
     def all_products(row, target, halo_target):
         summed = target[row]
         for slot in range(1, SLOTS):
-            summed = summed + halo_target[arrived_ref[row * SLOTS + slot]]
+            summed = summed + halo_target[table_s[LANES + 1, 0, slot * dev_rows + row]]
         return summed
 
     node_real = jnp.float32(0.0)
@@ -265,9 +303,8 @@
         core_copies[batch].wait_recv()
         mixed[batch] = share[batch, my_core] + from_core[batch]
         if batch < batches - 1:
-            to_y[batch] = mixed[batch].astype(to_y.dtype)
             copy = pltpu.make_async_remote_copy(
-                src_ref=to_y.at[batch],
+                src_ref=mixed.at[batch],
                 dst_ref=from_y.at[batch],
                 send_sem=y_send.at[batch],
                 recv_sem=y_recv.at[batch],
@@ -309,8 +346,8 @@
                         jnp.bfloat16
                     )
                 else:
-                    out_real = (node_real * real - node_imag * imag) / node_count
-                    out_imag = (node_real * imag + node_imag * real) / node_count
+                    out_real = node_real * real - node_imag * imag
+                    out_imag = node_real * imag + node_imag * real
                     for core in range(2):
                         at = core * chunk
                         share[batch, core, row, 0:chunk] = out_real[at : at + chunk]
@@ -343,7 +380,7 @@
     for row in range(dev_rows):
         total = mixed[batches - 1, row]
         for batch in range(batches - 1):
-            total = total + from_y[batch, row].astype(jnp.float32)
+            total = total + from_y[batch, row]
         out_ref[:, row, :] = total
     for copy in pending:
         copy.wait_send()
@@ -356,9 +393,7 @@
     width = col_count // batches
     chunk = width // 2
     entries = dev_rows * SLOTS
-    tables = index_tables(neighbours, dev_rows, peer_count)
     half, full = jnp.bfloat16, jnp.float32
-    smem = pl.BlockSpec(memory_space=pltpu.SMEM)
     vmem = pl.BlockSpec(memory_space=pltpu.VMEM)
     anywhere = pl.BlockSpec(memory_space=pl.ANY)
     dma = pltpu.SemaphoreType.DMA
@@ -367,8 +402,12 @@
         pltpu.VMEM((entries, block, 2 * block), half),
         pltpu.VMEM((dev_rows, block, 2 * block), half),
         pltpu.VMEM((col_count, dev_rows, block), full),
-        pltpu.VMEM((LANES, 1, HMAX), jnp.int32),
-        pltpu.SMEM((LANES, 1, HMAX), jnp.int32),
+        pltpu.VMEM((8, 128), jnp.int32),
+        pltpu.VMEM((LANES + 2, 8, 128), jnp.int32),
+        pltpu.SMEM((LANES + 2, 8, 128), jnp.int32),
+        pltpu.VMEM((LANES, 8, 128), jnp.int32),
+        pltpu.VMEM((LANES, 8, 128), jnp.int32),
+        pltpu.SMEM((LANES, 8, 128), jnp.int32),
         pltpu.VMEM((dev_rows + 1, col_count, block), half),
         pltpu.VMEM((HALO, col_count, block), half),
         pltpu.VMEM((HALO, col_count, block), half),
@@ -384,9 +423,9 @@
         pltpu.VMEM((batches, 2, dev_rows, 2 * chunk, block), full),
         pltpu.VMEM((batches, dev_rows, 2 * chunk, block), full),
         pltpu.VMEM((batches, dev_rows, 2 * chunk, block), full),
-        pltpu.VMEM((crossings, dev_rows, 2 * chunk, block), half),
-        pltpu.VMEM((crossings, dev_rows, 2 * chunk, block), half),
+        pltpu.VMEM((crossings, dev_rows, 2 * chunk, block), full),
         dma((4,)),
+        dma,
         dma,
         dma((LANES,)),
         dma((LANES,)),
@@ -400,20 +439,20 @@
     summed = pl.pallas_call(
         functools.partial(kernel, peer_count, node_count),
         out_shape=jax.ShapeDtypeStruct((2 * chunk, dev_rows, block), full),
-        in_specs=[smem, smem, smem, vmem, vmem, anywhere, anywhere, anywhere],
+        in_specs=[vmem, vmem, anywhere, anywhere, anywhere],
         out_specs=vmem,
         scratch_shapes=scratch,
         compiler_params=pltpu.CompilerParams(
             collective_id=0, has_side_effects=True, vmem_limit_bytes=60 * 1024 * 1024
         ),
     )(
-        *tables,
+        neighbours.T,
         columns,
         pencil_e.reshape(entries, block, block),
         pencil_a.reshape(entries, block, block),
         precond.reshape(2, dev_rows, block, block),
     )
-    return summed.reshape(2, chunk, dev_rows, block)
+    return summed.reshape(2, chunk, dev_rows, block) * (1.0 / node_count)
 
 
 def solution(mesh):

time: 53.2 us -> 48.2 us (0.906)
  local copies, waits for them, and re-layouts: 3.14 us -> 0 us
  Pallas kernels: 48.4 us -> 46.2 us
    unnamed x2 -> x0, local copies, waits for them, and re-layouts: 2.38 us -> none
    pallas_call x1, Pallas kernels: 48.4 us -> 46.2 us  [per_device(): pl.pallas_call(functools.partial(kernel, peer_count, node_count), out_sha...]
    mul x0 -> x1, other arithmetic: none -> 1.62 us  [per_device(): return summed.reshape(2, chunk, dev_rows, block) * (1.0 / node_count)]
    reduce_sum x2 -> x0, other arithmetic: 0.8 us -> none  [the longest x1 0.63 us: index_tables(): wanted = jnp.sum(jnp.where(matched, local[None, :], 0), axis=1)]
    reshape x2 -> x0, local copies, waits for them, and re-layouts: 0.75 us -> none  [the longest x1 0.66 us: index_tables(): return (own, arrived, entry, wanted.reshape(LANES, 1, HMAX))]
    select_n x2 -> x0, other arithmetic: 0.62 us -> none  [the longest x1 0.6 us: index_tables(): arrived = jnp.where(remote, place, HALO)]
where the time goes in v3:
time: 48.2 us; the launch traced here: 47.9 us
  Pallas kernels  46.2 us (96%)
  other arithmetic  1.62 us (3%)
    pallas_call x1, Pallas kernels, per_device(): pl.pallas_call(functools.partial(kernel, peer_count, node_count), out_sha...  46.2 us
    mul x1, other arithmetic, per_device(): return summed.reshape(2, chunk, dev_rows, block) * (1.0 / node_count)  1.62 us

profile of v3, /device:TPU:0, one launch (start us, length us, event | category | flops | bytes accessed | tf_op | source)
XLA Modules:
  0.0 47.9 jit_solution(11613487780080223567)
XLA Ops:
  0.0 46.2 %shard_map.55 = f32[16,24,128]{2,1,0:T(8,128)} custom-call(s32[5,24]{1,0:T(8,128)} %bitcast.8, bf16[32,24,128]{2,1,0:T(8,128)(2,1)} %cols_ref.1, bf16[120,128,128]{2,1,0:T(8,128)(2,1)} %bitcast.5, bf16[120,128,128]{2,1,0:T(8,128)(2,1)} %bitcast.6, bf16[2,24,128,128]{3,2,1,0:T(8,128)(2,1)} %bitcast.7), custom_call_target="tpu_custom_call" | custom-call | tf_op jit(solution)/shard_map/pallas_call | solution.py:439
  46.2 1.6 %broadcast_multiply_fusion = f32[16,24,128]{2,1,0:T(8,128)} fusion(f32[16,24,128]{2,1,0:T(8,128)} %shard_map.55), kind=kLoop, calls=%fused_computation | loop fusion | flops 49152 | bytes 393216 | tf_op jit(solution)/shard_map/mul | solution.py:455

commit v4 on v3

--- a/solution.py
+++ b/solution.py
@@ -120,10 +120,7 @@
     y_send,
     y_recv,
 ):
-    dev_rows = rhs.shape[0]
-    block = rhs.shape[2]
-    batches = vec.shape[1]
-    width = vec.shape[3] // 2
+    batches, dev_rows, width, block = rhs.shape
     chunk = width // 2
     offsets = lane_offsets(peer_count)
     me = lax.axis_index("rows")
@@ -176,11 +173,11 @@
                 jnp.bfloat16
             )
     vec_0[dev_rows] = jnp.zeros(vec_0.shape[1:], vec_0.dtype)
-    prod_0[HALO] = jnp.zeros(prod_0.shape[1:], prod_0.dtype)
     for batch in range(batches):
+        prod_0[batch, HALO] = jnp.zeros(prod_0.shape[2:], prod_0.dtype)
         prod[batch, HALO] = jnp.zeros(prod.shape[2:], prod.dtype)
-        for sweep in range(SWEEPS):
-            vec[sweep, batch, dev_rows] = jnp.zeros(vec.shape[3:], vec.dtype)
+    for sweep in range(SWEEPS):
+        vec[sweep, dev_rows] = jnp.zeros(vec.shape[2:], vec.dtype)
 
     pl.semaphore_wait(barrier, LANES + node_count - 1)
 
@@ -203,11 +200,13 @@
     to_scalars.wait()
     to_table.wait()
 
-    def send_halo(phase, source, leaving, arriving):
+    def send_halo(phase, source, batch, rows, leaving, arriving):
         copies = [None] * LANES
         for lane in (4, 0, 3, 1, 2):
             for rank in range(HMAX):
-                leaving[lane * HMAX + rank] = source[asked_s[lane, rank, 0]]
+                leaving[lane * HMAX + rank] = source[
+                    asked_s[lane, rank, 0], batch * rows : (batch + 1) * rows
+                ]
             here = pl.ds(lane * HMAX, HMAX)
             copy = pltpu.make_async_remote_copy(
                 src_ref=leaving.at[here],
@@ -250,8 +249,8 @@
                 matrix = weights[table_s[lane, rank, 0], :, 0:columns]
                 target[at] = jnp.dot(arriving[at], matrix, preferred_element_type=jnp.float32)
 
-    def all_products(row, target, halo_target):
-        summed = target[row]
+    def all_products(row, target, batch, rows, halo_target):
+        summed = target[row, batch * rows : (batch + 1) * rows]
         for slot in range(1, SLOTS):
             summed = summed + halo_target[table_s[LANES + 1, 0, slot * dev_rows + row]]
         return summed
@@ -263,37 +262,36 @@
         node_real = jnp.where(node == index, jnp.float32(math.cos(angle)), node_real)
         node_imag = jnp.where(node == index, jnp.float32(math.sin(angle)), node_imag)
 
-    copies = send_halo(0, vec_0, send_0, halo_0)
+    def phase_of(sweep, batch):
+        return (1 + sweep) * batches + batch
+
+    flights = {}
+    for batch in range(batches):
+        flights[-1, batch] = send_halo(
+            phase_of(-1, batch), vec_0, batch, width, send_0.at[batch], halo_0.at[batch]
+        )
     load_e.wait()
     own_products(vec_0, block, part_0)
     load_a.wait()
-    halo_products(copies, halo_0, block, prod_0)
     for copy in load_p:
         copy.wait()
 
-    def right_rows(row):
-        rhs[row] = all_products(row, part_0, prod_0)
-
-    row_loop(right_rows)
-
-    def phase_of(sweep, batch):
-        return 1 + sweep * batches + batch
-
-    flights = {}
     for batch in range(batches):
+        halo_products(flights[-1, batch], halo_0.at[batch], block, prod_0.at[batch])
 
         def first_rows(row, batch=batch):
-            right = rhs[row, batch * width : (batch + 1) * width]
+            right = all_products(row, part_0, batch, width, prod_0.at[batch])
+            rhs[batch, row] = right
             both = jnp.dot(
                 right.astype(jnp.bfloat16), inverse[row], preferred_element_type=jnp.float32
             )
             fresh = jnp.concatenate([both[:, 0:block], both[:, block:]], axis=0)
             iterate[batch, row] = fresh
-            vec[0, batch, row] = fresh.astype(jnp.bfloat16)
+            vec[0, row, batch * 2 * width : (batch + 1) * 2 * width] = fresh.astype(jnp.bfloat16)
 
         row_loop(first_rows)
         flights[0, batch] = send_halo(
-            phase_of(0, batch), vec.at[0, batch], outgoing.at[0, batch], halo.at[0, batch]
+            phase_of(0, batch), vec.at[0], batch, 2 * width, outgoing.at[0, batch], halo.at[0, batch]
         )
 
     core_copies = []
@@ -316,19 +314,18 @@
             pending.append(copy)
 
     for sweep in range(SWEEPS):
+        own_products(vec.at[sweep], 2 * block, part)
         for batch in range(batches):
-            source, arriving = vec.at[sweep, batch], halo.at[sweep, batch]
-            target, halo_target = part.at[batch], prod.at[batch]
-            own_products(source, 2 * block, target)
+            arriving, halo_target = halo.at[sweep, batch], prod.at[batch]
             if sweep == SWEEPS - 1 and batch > 0:
                 finish_core(batch - 1)
             halo_products(flights[sweep, batch], arriving, 2 * block, halo_target)
 
-            def sweep_rows(row, sweep=sweep, batch=batch, target=target, halo_target=halo_target):
-                both = all_products(row, target, halo_target)
+            def sweep_rows(row, sweep=sweep, batch=batch, halo_target=halo_target):
+                both = all_products(row, part, batch, 2 * width, halo_target)
                 e_real, a_real = both[:width, :block], both[:width, block:]
                 e_imag, a_imag = both[width:, :block], both[width:, block:]
-                right = rhs[row, batch * width : (batch + 1) * width]
+                right = rhs[batch, row]
                 res_real = right - (node_real * e_real - node_imag * e_imag - a_real)
                 res_imag = -(node_real * e_imag + node_imag * e_real - a_imag)
                 residual = jnp.concatenate([res_real, res_imag], axis=0).astype(jnp.bfloat16)
@@ -342,8 +339,8 @@
                 if sweep < SWEEPS - 1:
                     iterate[batch, row, 0:width] = real
                     iterate[batch, row, width : 2 * width] = imag
-                    vec[sweep + 1, batch, row] = jnp.concatenate([real, imag], axis=0).astype(
-                        jnp.bfloat16
+                    vec[sweep + 1, row, batch * 2 * width : (batch + 1) * 2 * width] = (
+                        jnp.concatenate([real, imag], axis=0).astype(jnp.bfloat16)
                     )
                 else:
                     out_real = node_real * real - node_imag * imag
@@ -357,7 +354,9 @@
             if sweep < SWEEPS - 1:
                 flights[sweep + 1, batch] = send_halo(
                     phase_of(sweep + 1, batch),
-                    vec.at[sweep + 1, batch],
+                    vec.at[sweep + 1],
+                    batch,
+                    2 * width,
                     outgoing.at[sweep + 1, batch],
                     halo.at[sweep + 1, batch],
                 )
@@ -409,15 +408,15 @@
         pltpu.VMEM((LANES, 8, 128), jnp.int32),
         pltpu.SMEM((LANES, 8, 128), jnp.int32),
         pltpu.VMEM((dev_rows + 1, col_count, block), half),
-        pltpu.VMEM((HALO, col_count, block), half),
-        pltpu.VMEM((HALO, col_count, block), half),
+        pltpu.VMEM((batches, HALO, width, block), half),
+        pltpu.VMEM((batches, HALO, width, block), half),
         pltpu.VMEM((dev_rows, col_count, block), full),
-        pltpu.VMEM((HALO + 1, col_count, block), full),
-        pltpu.VMEM((dev_rows, col_count, block), full),
-        pltpu.VMEM((SWEEPS, batches, dev_rows + 1, 2 * width, block), half),
+        pltpu.VMEM((batches, HALO + 1, width, block), full),
+        pltpu.VMEM((batches, dev_rows, width, block), full),
+        pltpu.VMEM((SWEEPS, dev_rows + 1, 2 * col_count, block), half),
         pltpu.VMEM((SWEEPS, batches, HALO, 2 * width, block), half),
         pltpu.VMEM((SWEEPS, batches, HALO, 2 * width, block), half),
-        pltpu.VMEM((batches, dev_rows, 2 * width, 2 * block), full),
+        pltpu.VMEM((dev_rows, 2 * col_count, 2 * block), full),
         pltpu.VMEM((batches, HALO + 1, 2 * width, 2 * block), full),
         pltpu.VMEM((batches, dev_rows, 2 * width, block), full),
         pltpu.VMEM((batches, 2, dev_rows, 2 * chunk, block), full),
@@ -429,8 +428,8 @@
         dma,
         dma((LANES,)),
         dma((LANES,)),
-        dma((1 + SWEEPS * batches, LANES)),
-        dma((1 + SWEEPS * batches, LANES)),
+        dma(((1 + SWEEPS) * batches, LANES)),
+        dma(((1 + SWEEPS) * batches, LANES)),
         dma((batches,)),
         dma((batches,)),
         dma((crossings,)),

time: 48.2 us -> 46.3 us (0.961)
  the two profiles are of different devices: /device:TPU:0 before, /device:TPU:21 now
where the time goes in v4:
time: 46.3 us; the launch traced here: 46.1 us
  Pallas kernels  44.5 us (96%)
  other arithmetic  1.62 us (3%)
    pallas_call x1, Pallas kernels, per_device(): pl.pallas_call(functools.partial(kernel, peer_count, node_count), out_sha...  44.5 us
    mul x1, other arithmetic, per_device(): return summed.reshape(2, chunk, dev_rows, block) * (1.0 / node_count)  1.62 us

profile of v4, /device:TPU:21, one launch (start us, length us, event | category | flops | bytes accessed | tf_op | source)
XLA Modules:
  0.0 46.1 jit_solution(13115382535314826833)
XLA Ops:
  0.0 44.5 %shard_map.55 = f32[16,24,128]{2,1,0:T(8,128)} custom-call(s32[5,24]{1,0:T(8,128)} %bitcast.8, bf16[32,24,128]{2,1,0:T(8,128)(2,1)} %cols_ref.1, bf16[120,128,128]{2,1,0:T(8,128)(2,1)} %bitcast.5, bf16[120,128,128]{2,1,0:T(8,128)(2,1)} %bitcast.6, bf16[2,24,128,128]{3,2,1,0:T(8,128)(2,1)} %bitcast.7), custom_call_target="tpu_custom_call" | custom-call | tf_op jit(solution)/shard_map/pallas_call | solution.py:438
  44.5 1.6 %broadcast_multiply_fusion = f32[16,24,128]{2,1,0:T(8,128)} fusion(f32[16,24,128]{2,1,0:T(8,128)} %shard_map.55), kind=kLoop, calls=%fused_computation | loop fusion | flops 49152 | bytes 393216 | tf_op jit(solution)/shard_map/mul | solution.py:454

commit v5 on v4

--- a/solution.py
+++ b/solution.py
@@ -165,6 +165,20 @@
     to_table = pltpu.make_async_copy(table_v, table_s, table_sem)
     to_table.start()
 
+    pl.semaphore_wait(barrier, LANES + node_count - 1)
+
+    pending = []
+    for lane, offset in enumerate(offsets):
+        copy = pltpu.make_async_remote_copy(
+            src_ref=want_v.at[lane],
+            dst_ref=asked_v.at[lane],
+            send_sem=want_send.at[lane],
+            recv_sem=want_recv.at[lane],
+            device_id={"rows": behind(offset)},
+            device_id_type=MESH,
+        )
+        copy.start()
+        pending.append(copy)
     wide_cols[...] = cols_ref[...].astype(jnp.float32)
     for row in range(dev_rows):
         for batch in range(batches):
@@ -179,20 +193,6 @@
     for sweep in range(SWEEPS):
         vec[sweep, dev_rows] = jnp.zeros(vec.shape[2:], vec.dtype)
 
-    pl.semaphore_wait(barrier, LANES + node_count - 1)
-
-    pending = []
-    for lane, offset in enumerate(offsets):
-        copy = pltpu.make_async_remote_copy(
-            src_ref=want_v.at[lane],
-            dst_ref=asked_v.at[lane],
-            send_sem=want_send.at[lane],
-            recv_sem=want_recv.at[lane],
-            device_id={"rows": behind(offset)},
-            device_id_type=MESH,
-        )
-        copy.start()
-        pending.append(copy)
     for copy in pending:
         copy.wait_recv()
     to_scalars = pltpu.make_async_copy(asked_v, asked_s, asked_sem)
@@ -298,7 +298,8 @@
     y_copies = []
 
     def finish_core(batch):
-        core_copies[batch].wait_recv()
+        for copy in core_copies[batch]:
+            copy.wait_recv()
         mixed[batch] = share[batch, my_core] + from_core[batch]
         if batch < batches - 1:
             copy = pltpu.make_async_remote_copy(
@@ -350,7 +351,24 @@
                         share[batch, core, row, 0:chunk] = out_real[at : at + chunk]
                         share[batch, core, row, chunk : 2 * chunk] = out_imag[at : at + chunk]
 
-            row_loop(sweep_rows)
+            if sweep == SWEEPS - 1:
+                core_copies.append([])
+            for third in range(dev_rows // ROW_STEP):
+                for inner in range(ROW_STEP):
+                    sweep_rows(third * ROW_STEP + inner)
+                if sweep == SWEEPS - 1:
+                    here = pl.ds(third * ROW_STEP, ROW_STEP)
+                    copy = pltpu.make_async_remote_copy(
+                        src_ref=share.at[batch, 1 - my_core, here],
+                        dst_ref=from_core.at[batch, here],
+                        send_sem=core_send.at[batch, third],
+                        recv_sem=core_recv.at[batch, third],
+                        device_id={"node": 2 * my_y + (1 - my_core)},
+                        device_id_type=MESH,
+                    )
+                    copy.start()
+                    core_copies[batch].append(copy)
+                    pending.append(copy)
             if sweep < SWEEPS - 1:
                 flights[sweep + 1, batch] = send_halo(
                     phase_of(sweep + 1, batch),
@@ -360,18 +378,6 @@
                     outgoing.at[sweep + 1, batch],
                     halo.at[sweep + 1, batch],
                 )
-            else:
-                copy = pltpu.make_async_remote_copy(
-                    src_ref=share.at[batch, 1 - my_core],
-                    dst_ref=from_core.at[batch],
-                    send_sem=core_send.at[batch],
-                    recv_sem=core_recv.at[batch],
-                    device_id={"node": 2 * my_y + (1 - my_core)},
-                    device_id_type=MESH,
-                )
-                copy.start()
-                core_copies.append(copy)
-                pending.append(copy)
 
     finish_core(batches - 1)
     for copy in y_copies:
@@ -430,8 +436,8 @@
         dma((LANES,)),
         dma(((1 + SWEEPS) * batches, LANES)),
         dma(((1 + SWEEPS) * batches, LANES)),
-        dma((batches,)),
-        dma((batches,)),
+        dma((batches, dev_rows // ROW_STEP)),
+        dma((batches, dev_rows // ROW_STEP)),
         dma((crossings,)),
         dma((crossings,)),
     ]

time: 46.3 us -> 46.1 us (level)
  the two profiles are of different devices: /device:TPU:21 before, /device:TPU:0 now
where the time goes in v5:
time: 46.1 us; the launch traced here: 45.5 us
  Pallas kernels  43.8 us (95%)
  other arithmetic  1.62 us (4%)
    pallas_call x1, Pallas kernels, per_device(): pl.pallas_call(functools.partial(kernel, peer_count, node_count), out_sha...  43.8 us
    mul x1, other arithmetic, per_device(): return summed.reshape(2, chunk, dev_rows, block) * (1.0 / node_count)  1.62 us

profile of v5, /device:TPU:0, one launch (start us, length us, event | category | flops | bytes accessed | tf_op | source)
XLA Modules:
  0.0 45.5 jit_solution(12575778051049017179)
XLA Ops:
  0.0 43.8 %shard_map.55 = f32[16,24,128]{2,1,0:T(8,128)} custom-call(s32[5,24]{1,0:T(8,128)} %bitcast.8, bf16[32,24,128]{2,1,0:T(8,128)(2,1)} %cols_ref.1, bf16[120,128,128]{2,1,0:T(8,128)(2,1)} %bitcast.5, bf16[120,128,128]{2,1,0:T(8,128)(2,1)} %bitcast.6, bf16[2,24,128,128]{3,2,1,0:T(8,128)(2,1)} %bitcast.7), custom_call_target="tpu_custom_call" | custom-call | tf_op jit(solution)/shard_map/pallas_call | solution.py:444
  43.8 1.6 %broadcast_multiply_fusion = f32[16,24,128]{2,1,0:T(8,128)} fusion(f32[16,24,128]{2,1,0:T(8,128)} %shard_map.55), kind=kLoop, calls=%fused_computation | loop fusion | flops 49152 | bytes 393216 | tf_op jit(solution)/shard_map/mul | solution.py:460

commit v6 on v5

--- a/solution.py
+++ b/solution.py
@@ -448,7 +448,7 @@
         out_specs=vmem,
         scratch_shapes=scratch,
         compiler_params=pltpu.CompilerParams(
-            collective_id=0, has_side_effects=True, vmem_limit_bytes=60 * 1024 * 1024
+            collective_id=0, has_side_effects=True, vmem_limit_bytes=53 * 1024 * 1024
         ),
     )(
         neighbours.T,

time: 46.1 us -> 45.2 us (0.980)
  local copies, waits for them, and re-layouts: 0 us -> 1.61 us
  Pallas kernels: 43.8 us -> 42.2 us
  other arithmetic: 1.62 us -> 0.69 us
    pallas_call x1, Pallas kernels: 43.8 us -> 42.2 us  [per_device(): pl.pallas_call(functools.partial(kernel, peer_count, node_count), out_sha...]
    unnamed x0 -> x4, local copies, waits for them, and re-layouts: none -> 1.61 us
    mul x1, other arithmetic: 1.62 us -> 0.69 us  [per_device(): return summed.reshape(2, chunk, dev_rows, block) * (1.0 / node_count)]
where the time goes in v6:
time: 45.2 us; the launch traced here: 44.5 us
  Pallas kernels  42.2 us (93%)
  local copies, waits for them, and re-layouts  1.61 us (4%)
  other arithmetic  0.69 us (2%)
    pallas_call x1, Pallas kernels, per_device(): pl.pallas_call(functools.partial(kernel, peer_count, node_count), out_sha...  42.2 us
    unnamed x4, local copies, waits for them, and re-layouts  1.61 us

profile of v6, /device:TPU:0, one launch (start us, length us, event | category | flops | bytes accessed | tf_op | source)
XLA Modules:
  0.0 44.5 jit_solution(13101983610046746911)
XLA Ops:
  0.0 0.0 copy-start
  0.0 0.9 %copy-done = bf16[32,24,128]{2,1,0:T(8,128)(2,1)S(1)} copy-done((bf16[32,24,128]{2,1,0:T(8,128)(2,1)S(1)}, bf16[32,24,128]{2,1,0:T(8,128)(2,1)}, u32[]{:S(2)}) %copy-start) | copy-done | bytes 196632
  0.9 0.0 copy-start.1
  0.9 0.7 %copy-done.1 = s32[24,5]{0,1:T(8,128)S(1)} copy-done((s32[24,5]{0,1:T(8,128)S(1)}, s32[24,5]{0,1:T(8,128)}, u32[]{:S(2)}) %copy-start.1) | copy-done | bytes 504
  1.6 42.2 %shard_map.55 = f32[16,24,128]{2,1,0:T(8,128)S(1)} custom-call(s32[5,24]{1,0:T(8,128)S(1)} %bitcast.5, bf16[32,24,128]{2,1,0:T(8,128)(2,1)S(1)} %copy-done, bf16[120,128,128]{2,1,0:T(8,128)(2,1)} %bitcast.6, bf16[120,128,128]{2,1,0:T(8,128)(2,1)} %bitcast.7, bf16[2,24,128,128]{3,2,1,0:T(8,128)(2,1)} %bitcast.8), custom_call_target="tpu_custom_call" | custom-call | tf_op jit(solution)/shard_map/pallas_call | solution.py:444
  43.8 0.7 %broadcast_multiply_fusion = f32[16,24,128]{2,1,0:T(8,128)} fusion(f32[16,24,128]{2,1,0:T(8,128)S(1)} %shard_map.55), kind=kLoop, calls=%fused_computation | loop fusion | flops 49152 | bytes 393216 | tf_op jit(solution)/shard_map/mul | solution.py:460
Async XLA Ops:
  0.0 0.9 %copy-start = (bf16[32,24,128]{2,1,0:T(8,128)(2,1)S(1)}, bf16[32,24,128]{2,1,0:T(8,128)(2,1)}, u32[]{:S(2)}) copy-start(bf16[32,24,128]{2,1,0:T(8,128)(2,1)} %cols_ref.1) | copy-start | bytes 589828
  0.9 0.7 %copy-start.1 = (s32[24,5]{0,1:T(8,128)S(1)}, s32[24,5]{0,1:T(8,128)}, u32[]{:S(2)}) copy-start(s32[24,5]{0,1:T(8,128)} %param.9) | copy-start | bytes 1444
